TPU v7x, 512 devices: a whole 4x4x16 slice. The times are simulated.
512 devices in a mesh: ctx: 32 (over z, core), head: 16 (over y, x).
Axes of the slice: x: 4, y: 4, z: 16, core: 2. Of those that a mesh axis runs over, the one named last changes fastest.
Arguments:
- queries: bfloat16 [8192, 8192], P('ctx', 'head'), may hold values from -6 to 6
- keys: bfloat16 [8192, 8192], P('ctx', 'head'), may hold values from -6 to 6
- values: bfloat16 [8192, 8192], P('ctx', 'head'), may hold values from -6 to 6
- out_weight: bfloat16 [8192, 6144], P('head', 'ctx'), may hold values from -0.0625 to 0.0625
Outputs:
- output: bfloat16 [8192, 6144], P('ctx', 'head')
All inputs are finite; a program needn't handle non-finite values.
Results may differ from a plain program's by a relative error of at most 0.022.
Values may be sent and summed in bfloat16 or wider, within the bound.
No kernel may reach another device: no remote copies, remote signals or barrier semaphores. Data moves between devices by JAX's collectives and lax.ppermute only.
A program may use at most 64 MiB of HBM per device.

v0:
```python
import jax
import jax.numpy as jnp
from jax import lax
from jax.sharding import PartitionSpec as P

DH = 128


def carried_in(shard, axis, combine, identity):
    length, index = (lax.axis_size(axis), lax.axis_index(axis))
    everything = lax.all_gather(shard.astype(jnp.bfloat16), axis)
    start = jnp.broadcast_to(jnp.asarray(identity, shard.dtype), shard.shape)

    def turn(k, before):
        reached = k < index
        new = combine(before, everything[k].astype(shard.dtype))
        return jnp.where(reached, new, before)

    return lax.fori_loop(0, length, turn, start)


def per_device(queries, keys, values, out_weight):
    tok_rows, width = queries.shape
    local_heads = width // DH
    q = queries.reshape(tok_rows, local_heads, DH)
    k = keys.reshape(tok_rows, local_heads, DH)
    v = values.reshape(tok_rows, local_heads, DH)
    state = jnp.einsum("thd,the->hde", k, v, preferred_element_type=jnp.float32).astype(
        jnp.bfloat16
    )

    def add_states(earlier, later):
        return earlier + later

    summed = carried_in(
        state.astype(jnp.float32), "ctx", add_states, jnp.zeros(state.shape, jnp.float32)
    )
    prefix = summed.astype(jnp.bfloat16)
    scores = jnp.einsum("thd,shd->hts", q, k, preferred_element_type=jnp.float32)
    rows = jnp.arange(tok_rows, dtype=jnp.int32)
    causal = rows[:, None] >= rows[None, :]
    scores = jnp.where(causal[None], scores, 0.0).astype(jnp.bfloat16)
    intra = jnp.einsum("hts,she->the", scores, v, preferred_element_type=jnp.float32)
    inter = jnp.einsum("thd,hde->the", q, prefix, preferred_element_type=jnp.float32)
    position = (lax.axis_index("ctx") * tok_rows + rows).astype(jnp.float32)
    scale = jnp.sqrt(DH * (position + 1.0))
    attended = (
        ((intra + inter) / scale[:, None, None]).astype(jnp.bfloat16).reshape(tok_rows, width)
    )
    partial_sum = jnp.dot(
        attended,
        lax.all_gather(out_weight, "ctx", axis=1, tiled=True),
        preferred_element_type=jnp.float32,
    )
    rounded = partial_sum.astype(jnp.bfloat16).astype(jnp.float32)
    result = lax.psum_scatter(rounded.astype(jnp.bfloat16), "head", scatter_dimension=1, tiled=True)
    return result


def solution(mesh):
    return jax.shard_map(
        per_device,
        mesh=mesh,
        in_specs=(P("ctx", "head"), P("ctx", "head"), P("ctx", "head"), P("head", "ctx")),
        out_specs=P("ctx", "head"),
        check_vma=False,
    )
```

profile of v0, /device:TPU:1, one launch (start us, length us, event | category | flops | bytes accessed | tf_op | source)
XLA Modules:
  0.0 267.5 jit_solution(5935078673604531815)
XLA Ops:
  6.5 0.0 copy-start
  6.5 0.0 all-gather.6.cloned.1.call-start
  6.5 1.1 copy.16
  7.7 1.8 convolution_convert_fusion.1
  9.5 0.0 all-gather.6.cloned.1.call-update
  9.5 0.0 all-gather.4.cloned.1.call-start
  9.6 0.7 all-gather.4.cloned.1.call-update
  10.3 0.0 reduce-scatter.4.cloned.1.call-start
  10.4 78.8 %all-gather.6.cloned.1.call-done = bf16[128,128,128]{2,1,0:T(8,128)(2,1)} async-done(((bf16[4,128,128]{2,1,0:T(8,128)(2,1)}), bf16[128,128,128]{2,1,0:T(8,128)(2,1)}) %all-gather.6.cloned.1.call-update) | async-done | bytes 4194320 | tf_op jit(solution)/shard_map/all_gather | solution.py:11
  89.1 34.0 %while.14 = (s32[]{:T(128)}, f32[4,128,128]{2,1,0:T(8,128)S(1)}, s32[]{:T(128)}, bf16[32,4,128,128]{3,2,1,0:T(8,128)(2,1)}, s32[]{:T(128)}, /*index=5*/s32[]{:T(128)}) while((s32[]{:T(128)}, f32[4,128,128]{2,1,0:T(8,128)S(1)}, s32[]{:T(128)}, bf16[32,4,128,128]{3,2,1,0:T(8,128)(2,1)}, s32[]{:T(128)}, /*index=5*/s32[]{:T(128)}) %tuple.41), condition=%wide.region_1.2_spmd.clone, body=%wide.region_0.1_spmd.clone.sunk | while | flops 262148 | bytes 655453 | solution.py:19
  89.1 1.0 add_select_fusion.2
  90.2 1.0 add_select_fusion.2
  91.3 1.0 add_select_fusion.2
  92.3 1.0 add_select_fusion.2
  93.4 1.0 add_select_fusion.2
  94.4 1.0 add_select_fusion.2
  95.5 1.0 add_select_fusion.2
  96.6 1.0 add_select_fusion.2
  97.6 1.0 add_select_fusion.2
  98.7 1.0 add_select_fusion.2
  99.7 1.0 add_select_fusion.2
  100.8 1.0 add_select_fusion.2
  101.9 1.0 add_select_fusion.2
  102.9 1.0 add_select_fusion.2
  104.0 1.1 add_select_fusion.2
  105.1 1.0 add_select_fusion.2
  106.1 1.0 add_select_fusion.2
  107.2 1.0 add_select_fusion.2
  108.2 1.0 add_select_fusion.2
  109.3 1.1 add_select_fusion.2
  110.4 1.0 add_select_fusion.2
  111.4 1.0 add_select_fusion.2
  112.5 1.0 add_select_fusion.2
  113.6 1.0 add_select_fusion.2
  114.6 1.0 add_select_fusion.2
  115.7 1.0 add_select_fusion.2
  116.8 1.0 add_select_fusion.2
  117.8 1.0 add_select_fusion.2
  118.9 1.0 add_select_fusion.2
  120.0 1.0 add_select_fusion.2
  121.0 1.0 add_select_fusion.2
  122.1 1.0 add_select_fusion.2
  123.1 0.0 copy-done
  123.1 0.3 convolution_bitcast_fusion
  123.4 2.1 fusion.5
  125.5 40.0 %all-gather.4.cloned.1.call-done = bf16[512,6144]{0,1:T(8,128)(2,1)} async-done(((bf16[512,192]{0,1:T(8,128)(2,1)}), bf16[512,6144]{0,1:T(8,128)(2,1)}) %all-gather.4.cloned.1.call-update) | async-done | bytes 6291472 | tf_op jit(solution)/shard_map/all_gather | solution.py:52
  165.6 4.7 %convolution_convert_fusion = bf16[256,6144]{1,0:T(8,128)(2,1)S(1)} fusion(bf16[256,512]{0,1:T(8,128)(2,1)} %bitcast.53, bf16[512,6144]{0,1:T(8,128)(2,1)} %all-gather.4.cloned.1.call-done), kind=kOutput, calls=%fused_computation.1 | convolution fusion | flops 1612185600 | bytes 9699328 | tf_op jit(solution)/shard_map/dot_general | solution.py:50
  170.3 2.8 %copy.17 = bf16[256,6144]{0,1:T(8,128)(2,1)} copy(bf16[256,6144]{1,0:T(8,128)(2,1)S(1)} %convolution_convert_fusion) | data formatting | bytes 6291456
  173.1 0.0 reduce-scatter.4.cloned.1.call-update
  173.1 86.1 %reduce-scatter.4.cloned.1.call-done = bf16[384,256]{1,0:T(8,128)(2,1)} async-done(((bf16[6144,256]{1,0:T(8,128)(2,1)}), bf16[384,256]{1,0:T(8,128)(2,1)}) %reduce-scatter.4.cloned.1.call-update) | async-done | bytes 196624
  259.2 1.7 copy.18
  (3 shorter events, 0.0 us)
Async XLA Ops:
  6.5 116.6 %copy-start = (bf16[256,512]{1,0:T(8,128)(2,1)S(1)}, bf16[256,512]{1,0:T(8,128)(2,1)}, u32[]{:S(2)}) copy-start(bf16[256,512]{1,0:T(8,128)(2,1)} %param.6) | copy-start | bytes 786436
  6.5 82.6 %all-gather.6.cloned.1.call-start = ((), (), s32[]{:S(2)}) async-start(), calls=%async_computation.2 | async-start | bytes 4325376 | tf_op jit(solution)/shard_map/all_gather | solution.py:11
  9.5 156.0 %all-gather.4.cloned.1.call-start = ((), (), s32[]{:S(2)}) async-start(), calls=%async_computation.1 | async-start | bytes 6488064 | tf_op jit(solution)/shard_map/all_gather | solution.py:52
  10.3 248.9 %reduce-scatter.4.cloned.1.call-start = ((), (), s32[]{:S(2)}) async-start(), calls=%async_computation.3 | async-start | bytes 3342336
Sparse Core Ops, SparseCore 0:
  9.6 79.4 all-gather.5
  91.3 74.2 all-gather.3
  173.2 85.9 reduce-scatter.3
where the time goes:
time: 269 us; the launch traced here: 267 us
  waiting for transfers between devices  206 us (77%)
  other arithmetic  33.3 us (12%)
  between operations  13.2 us (5%)
  matrix products  8.95 us (3%)
  local copies, waits for them, and re-layouts  5.66 us (2%)
    unnamed x4, waiting for transfers between devices  86.8 us
    all_gather x1, waiting for transfers between devices, carried_in(): everything = lax.all_gather(shard.astype(jnp.bfloat16), axis)  78.8 us
    all_gather x1, waiting for transfers between devices, per_device(): lax.all_gather(out_weight, 'ctx', axis=1, tiled=True)  40 us
    select_n x32, other arithmetic, turn(): return jnp.where(reached, new, before)  33.3 us
  transfers between devices with their start and end apart: 3, of which 3 were waited for; matrix products, arithmetic and copies ran while one was open for 13% of the time, Pallas kernels for 0%

commit v1 on v0

v1 whole, which is shorter than its diff:
```python
import functools

import jax
import jax.numpy as jnp
from jax import lax
from jax.experimental import pallas as pl
from jax.experimental.pallas import tpu as pltpu
from jax.sharding import Mesh
from jax.sharding import PartitionSpec as P

DH = 128
BF16 = jnp.bfloat16
F32 = jnp.float32
GRID = {"za": 4, "zb": 2, "zc": 2, "core": 2, "y": 4, "x": 4}
AXES = tuple(GRID)
CTX = ("za", "zb", "zc", "core")
HEAD = ("y", "x")
NEAR = ("zb", "zc", "core")
VMEM = pltpu.CompilerParams(vmem_limit_bytes=32 * 1024 * 1024)


def dot(a, b, dims):
    return lax.dot_general(a, b, (dims, ((), ())), preferred_element_type=F32)


def state_kernel(k_ref, v_ref, out_ref):
    for h in range(k_ref.shape[1] // DH):
        cols = pl.ds(h * DH, DH)
        out_ref[cols, :] = dot(k_ref[:, cols], v_ref[:, cols], ((0,), (0,))).astype(BF16)


def block_states(k, v):
    return pl.pallas_call(
        state_kernel,
        out_shape=jax.ShapeDtypeStruct((k.shape[1], DH), BF16),
        compiler_params=VMEM,
        name="block_state",
    )(k, v)


def attend_kernel(index_ref, q_ref, k_ref, v_ref, prefix_ref, out_ref):
    rows = q_ref.shape[0]
    causal = lax.broadcasted_iota(jnp.int32, (rows, rows), 0) >= lax.broadcasted_iota(
        jnp.int32, (rows, rows), 1
    )
    position = index_ref[0] * rows + lax.broadcasted_iota(jnp.int32, (rows, DH), 0)
    scale = jnp.sqrt(DH * (position.astype(F32) + 1.0))
    for h in range(q_ref.shape[1] // DH):
        cols = pl.ds(h * DH, DH)
        q = q_ref[:, cols]
        scores = jnp.where(causal, dot(q, k_ref[:, cols], ((1,), (1,))), 0.0).astype(BF16)
        both = dot(scores, v_ref[:, cols], ((1,), (0,))) + dot(q, prefix_ref[cols, :], ((1,), (0,)))
        attended = (both / scale).astype(BF16)
        for copy in range(out_ref.shape[0]):
            out_ref[copy, :, cols] = attended


def attend(index, q, k, v, prefix, copies):
    whole = pl.BlockSpec(memory_space=pltpu.VMEM)
    return pl.pallas_call(
        attend_kernel,
        out_shape=jax.ShapeDtypeStruct((copies, *q.shape), BF16),
        in_specs=[pl.BlockSpec(memory_space=pltpu.SMEM)] + [whole] * 4,
        out_specs=whole,
        compiler_params=VMEM,
        name="attend",
    )(index, q, k, v, prefix)


def project_kernel(w_ref, a_ref, out_ref):
    for t in range(a_ref.shape[0]):
        total = dot(w_ref[0, 0], a_ref[t, 0], ((1,), (1,)))
        for g in range(1, a_ref.shape[1]):
            total += dot(w_ref[0, g], a_ref[t, g], ((1,), (1,)))
        out_ref[t, 0] = total.astype(BF16)


def project(weight, attended):
    chunks, groups, columns, width = weight.shape
    blocks, _, tokens, _ = attended.shape
    return pl.pallas_call(
        project_kernel,
        grid=(chunks,),
        out_shape=jax.ShapeDtypeStruct((blocks, chunks, columns, tokens), BF16),
        in_specs=[
            pl.BlockSpec((1, groups, columns, width), lambda i: (i, 0, 0, 0)),
            pl.BlockSpec((blocks, groups, tokens, width), lambda i: (0, 0, 0, 0)),
        ],
        out_specs=pl.BlockSpec((blocks, 1, columns, tokens), lambda i: (0, i, 0, 0)),
        compiler_params=VMEM,
        name="project",
    )(weight, attended)


def finish_kernel(parts_ref, out_ref):
    halves, terms, columns, tokens = parts_ref.shape
    for half in range(halves):
        total = parts_ref[half, 0].astype(F32)
        for term in range(1, terms):
            total += parts_ref[half, term].astype(F32)
        out_ref[pl.ds(half * columns, columns), :] = total.astype(BF16)


def finish(parts):
    halves, _, columns, tokens = parts.shape
    return pl.pallas_call(
        finish_kernel,
        out_shape=jax.ShapeDtypeStruct((halves * columns, tokens), BF16),
        compiler_params=VMEM,
        name="finish",
    )(parts)


def flat(**at):
    index = 0
    for axis, size in GRID.items():
        index = index * size + at[axis]
    return index


def weight_moves():
    pairs = []
    for za in range(4):
        for zj in range(4):
            for core in range(2):
                for y in range(4):
                    for x in range(4):
                        source = flat(za=za, zb=zj // 2, zc=zj % 2, core=core, y=y, x=x)
                        target = flat(za=za, zb=x // 2, zc=core, core=x % 2, y=y, x=zj)
                        pairs.append((source, target))
    return pairs


def earlier_states(state):
    rows = state.shape[0] // 8
    pieces = lax.all_to_all(state.reshape(8, rows, DH), NEAR, 0, 0)
    pieces = pieces.astype(F32)
    running = jnp.cumsum(pieces, axis=0)
    total = running[-1]
    before = running - pieces
    totals = lax.all_gather(total.astype(BF16), "za").astype(F32)
    reached = jnp.arange(GRID["za"])[:, None, None] < lax.axis_index("za")
    carried = jnp.sum(jnp.where(reached, totals, 0.0), axis=0)
    prefix = (before + carried[None]).astype(BF16)
    return lax.all_to_all(prefix, NEAR, 0, 0).reshape(state.shape)


def per_device(queries, keys, values, out_weight):
    tokens, width = queries.shape
    columns = out_weight.shape[1]
    moved = lax.ppermute(out_weight.T, AXES, weight_moves())
    weight = lax.all_gather(moved, ("za", "zb", "core"))
    weight = weight.reshape(GRID["y"], GRID["x"], columns, width)

    prefix = earlier_states(block_states(keys, values))
    index = lax.axis_index(CTX).astype(jnp.int32).reshape(1)
    attended = attend(index, queries, keys, values, prefix, GRID["zc"] * GRID["x"])
    attended = lax.all_to_all(attended, ("zc", "x"), 0, 0)
    attended = attended.reshape(GRID["zc"], GRID["x"], tokens, width)
    partial = project(weight, attended)
    partial = partial.reshape(GRID["zc"] * GRID["y"], columns, tokens)
    parts = lax.all_to_all(partial, ("zc", "y"), 0, 0)
    return finish(parts.reshape(GRID["zc"], GRID["y"], columns, tokens)).T


def solution(mesh):
    grid = Mesh(mesh.devices.reshape(tuple(GRID.values())), AXES)
    spec = P(CTX, HEAD)
    return jax.shard_map(
        per_device,
        mesh=grid,
        in_specs=(spec, spec, spec, P(HEAD, CTX)),
        out_specs=spec,
        check_vma=False,
    )
```

time: 269 us -> 181 us (0.67)
  waiting for transfers between devices: 206 us -> 93.6 us
  blocking collectives: 0 us -> 33.5 us
  other arithmetic: 33.3 us -> 0.81 us
  starting transfers between devices: 0.08 us -> 26.6 us
  matrix products: 8.95 us -> 0 us
  Pallas kernels: 0 us -> 5.21 us
    unnamed x4 -> x1, waiting for transfers between devices: 86.8 us -> 0.02 us
    all_gather x2 -> x1, waiting for transfers between devices: 119 us -> 57.1 us  [per_device(): weight = lax.all_gather(moved, ('za', 'zb', 'core'))]
    select_n x32 -> x0, other arithmetic: 33.3 us -> none  [turn(): return jnp.where(reached, new, before)]
    ppermute x0 -> x1, waiting for transfers between devices: none -> 24.9 us  [per_device(): moved = lax.ppermute(out_weight.T, AXES, weight_moves())]
    all_to_all x0 -> x3, starting transfers between devices: none -> 22 us  [the longest x1 10.2 us: earlier_states(): pieces = lax.all_to_all(state.reshape(8, rows, DH), NEAR, 0, 0)]
    all_gather x0 -> x1, blocking collectives: none -> 17.5 us  [earlier_states(): totals = lax.all_gather(total.astype(BF16), 'za').astype(F32)]
    all_to_all x0 -> x1, blocking collectives: none -> 16.1 us  [per_device(): parts = lax.all_to_all(partial, ('zc', 'y'), 0, 0)]
    all_to_all x0 -> x3, waiting for transfers between devices: none -> 11.7 us  [the longest x1 5.84 us: earlier_states(): return lax.all_to_all(prefix, NEAR, 0, 0).reshape(state.shape)]
  transfers between devices with their start and end apart: 3 -> 5, of which waited for: 3 -> 4; matrix products, arithmetic and copies ran while one was open for 13% -> 0% of each run, Pallas kernels for 0% -> 0%
where the time goes in v1:
time: 181 us; the launch traced here: 180 us
  waiting for transfers between devices  93.6 us (52%)
  blocking collectives  33.5 us (19%)
  starting transfers between devices  26.6 us (15%)
  between operations  13.5 us (7%)
  local copies, waits for them, and re-layouts  6.65 us (4%)
  Pallas kernels  5.21 us (3%)
    all_gather x1, waiting for transfers between devices, per_device(): weight = lax.all_gather(moved, ('za', 'zb', 'core'))  57.1 us
    ppermute x1, waiting for transfers between devices, per_device(): moved = lax.ppermute(out_weight.T, AXES, weight_moves())  24.9 us
    all_gather x1, blocking collectives, earlier_states(): totals = lax.all_gather(total.astype(BF16), 'za').astype(F32)  17.5 us
    all_to_all x1, blocking collectives, per_device(): parts = lax.all_to_all(partial, ('zc', 'y'), 0, 0)  16.1 us
    all_to_all x1, starting transfers between devices, earlier_states(): pieces = lax.all_to_all(state.reshape(8, rows, DH), NEAR, 0, 0)  10.2 us
    all_to_all x1, starting transfers between devices, earlier_states(): return lax.all_to_all(prefix, NEAR, 0, 0).reshape(state.shape)  7.21 us
    all_to_all x1, waiting for transfers between devices, earlier_states(): return lax.all_to_all(prefix, NEAR, 0, 0).reshape(state.shape)  5.84 us
    all_to_all x1, waiting for transfers between devices, earlier_states(): pieces = lax.all_to_all(state.reshape(8, rows, DH), NEAR, 0, 0)  5.84 us
  transfers between devices with their start and end apart: 5, of which 4 were waited for; matrix products, arithmetic and copies ran while one was open for 0% of the time, Pallas kernels for 0%

profile of v1, /device:TPU:1, one launch (start us, length us, event | category | flops | bytes accessed | tf_op | source)
XLA Modules:
  0.0 180.0 jit_solution(10303762257396388978)
XLA Ops:
  6.5 0.0 copy-start.2
  6.5 0.9 copy-done.2
  7.5 0.0 copy-start.4
  7.5 0.9 copy-done.4
  8.4 0.0 copy-start.3
  8.4 0.0 copy-start.5
  8.4 0.0 copy-start.6
  8.4 0.9 block_state.1
  9.4 10.2 %all-to-all-start = ((bf16[8,64,128]{2,1,0:T(8,128)(2,1)}), bf16[8,64,128]{2,1,0:T(8,128)(2,1)S(1)}, u32[]{:S(2)}, u32[]{:S(2)}) async-start(bf16[8,64,128]{2,1,0:T(8,128)(2,1)} %bitcast.3), calls=%async_computation | async-start | bytes 262144 | tf_op jit(solution)/shard_map/all_to_all | solution.py:136
  19.5 5.8 %all-to-all-done = bf16[8,64,128]{2,1,0:T(8,128)(2,1)S(1)} async-done(((bf16[8,64,128]{2,1,0:T(8,128)(2,1)}), bf16[8,64,128]{2,1,0:T(8,128)(2,1)S(1)}, u32[]{:S(2)}, u32[]{:S(2)}) %all-to-all-start) | async-done | bytes 131104 | tf_op jit(solution)/shard_map/all_to_all | solution.py:136
  25.4 17.5 %all_gather.12 = bf16[4,64,128]{2,1,0:T(8,128)(2,1)S(1)} all-gather(bf16[1,64,128]{2,1,0:T(8,128)(2,1)S(1)} %slice.7), channel_id=1, replica_groups=mesh['za'=4,'zb'=2,'zc'=2,'core'=2,'y'=4,'x'=4] {'za'}, dimensions={0}, use_global_device_ids=true | all-gather | bytes 81920 | tf_op jit(solution)/shard_map/all_gather | solution.py:141
  42.9 0.1 select_reduce_fusion
  43.0 0.7 fusion.3
  43.7 7.2 %all-to-all-start.1 = ((bf16[8,64,128]{2,1,0:T(8,128)(2,1)}), bf16[8,64,128]{2,1,0:T(8,128)(2,1)S(1)}, u32[]{:S(2)}, u32[]{:S(2)}) async-start(bf16[8,64,128]{2,1,0:T(8,128)(2,1)} %fusion.3), calls=%async_computation.1 | async-start | bytes 262144 | tf_op jit(solution)/shard_map/all_to_all | solution.py:145
  50.9 5.8 %all-to-all-done.1 = bf16[8,64,128]{2,1,0:T(8,128)(2,1)S(1)} async-done(((bf16[8,64,128]{2,1,0:T(8,128)(2,1)}), bf16[8,64,128]{2,1,0:T(8,128)(2,1)S(1)}, u32[]{:S(2)}, u32[]{:S(2)}) %all-to-all-start.1) | async-done | bytes 131104 | tf_op jit(solution)/shard_map/all_to_all | solution.py:145
  56.7 0.0 copy-done.3
  56.7 0.0 copy-done.5
  56.7 0.0 copy-done.6
  56.7 0.8 attend.1
  57.5 0.0 copy-start
  57.6 1.4 copy-done
  58.9 0.0 copy-start.8
  58.9 4.6 %all-to-all-start.2 = ((bf16[8,256,512]{2,1,0:T(8,128)(2,1)}), bf16[8,256,512]{2,1,0:T(8,128)(2,1)S(1)}, u32[]{:S(2)}, u32[]{:S(2)}) async-start(bf16[8,256,512]{2,1,0:T(8,128)(2,1)} %copy-done), calls=%async_computation.2 | async-start | bytes 4194304 | tf_op jit(solution)/shard_map/all_to_all | solution.py:158
  63.5 0.0 all-gather.3.cloned.1.call-start
  63.6 0.0 copy-done.8
  63.6 4.6 %collective-permute-start = (bf16[192,512]{1,0:T(8,128)(2,1)S(1)}, bf16[192,512]{1,0:T(8,128)(2,1)S(1)}, u32[]{:S(2)}, u32[]{:S(2)}) collective-permute-start(bf16[192,512]{1,0:T(8,128)(2,1)S(1)} %bitcast.15), channel_id=1, source_target_pairs={{0,0},{1,16},{2,64},{3,80},{4,4},{5,20},{6,68},{7,84},{8,8},{9,24}... | collective-permute-start | bytes 589832 | tf_op jit(solution)/shard_map/ppermute | solution.py:151
  68.2 24.9 %collective-permute-done = bf16[192,512]{1,0:T(8,128)(2,1)S(1)} collective-permute-done((bf16[192,512]{1,0:T(8,128)(2,1)S(1)}, bf16[192,512]{1,0:T(8,128)(2,1)S(1)}, u32[]{:S(2)}, u32[]{:S(2)}) %collective-permute-start) | collective-permute-done | bytes 196640 | tf_op jit(solution)/shard_map/ppermute | solution.py:151
  93.1 0.0 copy-start.7
  93.1 0.7 copy-done.7
  93.8 0.0 all-gather.3.cloned.1.call-update
  93.8 57.1 %all-gather.3.cloned.1.call-done = bf16[3072,512]{1,0:T(8,128)(2,1)} async-done(((bf16[192,512]{1,0:T(8,128)(2,1)}), bf16[3072,512]{1,0:T(8,128)(2,1)}) %all-gather.3.cloned.1.call-update) | async-done | bytes 3145744 | tf_op jit(solution)/shard_map/all_gather | solution.py:152
  150.9 0.0 all-to-all-done.2
  150.9 0.0 copy-start.1
  150.9 1.9 %copy-done.1 = bf16[3072,512]{1,0:T(8,128)(2,1)S(1)} copy-done((bf16[3072,512]{1,0:T(8,128)(2,1)S(1)}, bf16[3072,512]{1,0:T(8,128)(2,1)}, u32[]{:S(2)}) %copy-start.1) | copy-done | bytes 3145752
  152.8 3.4 %project.1 = bf16[2,4,192,256]{3,2,1,0:T(8,128)(2,1)S(1)} custom-call(bf16[4,4,192,512]{3,2,1,0:T(8,128)(2,1)S(1)} %bitcast.10, bf16[2,4,256,512]{3,2,1,0:T(8,128)(2,1)S(1)} %bitcast.9), custom_call_target="tpu_custom_call" | custom-call | tf_op jit(solution)/shard_map/project/pallas_call | solution.py:81
  156.2 16.1 %all_to_all.20 = bf16[8,192,256]{2,1,0:T(8,128)(2,1)S(1)} all-to-all(bf16[8,192,256]{2,1,0:T(8,128)(2,1)S(1)} %bitcast.12), channel_id=1, replica_groups=mesh['za'=4,'zb'=2,'zc'=2,'core'=2,'y'=4,'x'=4] {'zc','y'}, dimensions={0} | all-to-all | bytes 1572864 | tf_op jit(solution)/shard_map/all_to_all | solution.py:162
  172.2 0.1 finish.1
  172.3 0.8 copy.6
  (3 shorter events, 0.0 us)
Async XLA Ops:
  6.5 0.9 copy-start.2
  7.5 0.9 copy-start.4
  8.4 48.3 %copy-start.3 = (bf16[256,512]{1,0:T(8,128)(2,1)S(1)}, bf16[256,512]{1,0:T(8,128)(2,1)}, u32[]{:S(2)}) copy-start(bf16[256,512]{1,0:T(8,128)(2,1)} %k_ref.3) | copy-start | bytes 786436
  8.4 48.3 %copy-start.5 = (bf16[256,512]{1,0:T(8,128)(2,1)S(1)}, bf16[256,512]{1,0:T(8,128)(2,1)}, u32[]{:S(2)}) copy-start(bf16[256,512]{1,0:T(8,128)(2,1)} %v_ref.3) | copy-start | bytes 786436
  8.4 48.3 %copy-start.6 = (bf16[256,512]{1,0:T(8,128)(2,1)S(1)}, bf16[256,512]{1,0:T(8,128)(2,1)}, u32[]{:S(2)}) copy-start(bf16[256,512]{1,0:T(8,128)(2,1)} %q_ref.1) | copy-start | bytes 786436
  9.4 16.0 %all-to-all-start = ((bf16[8,64,128]{2,1,0:T(8,128)(2,1)}), bf16[8,64,128]{2,1,0:T(8,128)(2,1)S(1)}, u32[]{:S(2)}, u32[]{:S(2)}) async-start(bf16[8,64,128]{2,1,0:T(8,128)(2,1)} %bitcast.3), calls=%async_computation | async-start | bytes 262144 | tf_op jit(solution)/shard_map/all_to_all | solution.py:136
  43.7 13.1 %all-to-all-start.1 = ((bf16[8,64,128]{2,1,0:T(8,128)(2,1)}), bf16[8,64,128]{2,1,0:T(8,128)(2,1)S(1)}, u32[]{:S(2)}, u32[]{:S(2)}) async-start(bf16[8,64,128]{2,1,0:T(8,128)(2,1)} %fusion.3), calls=%async_computation.1 | async-start | bytes 262144 | tf_op jit(solution)/shard_map/all_to_all | solution.py:145
  57.5 1.4 copy-start
  58.9 4.7 %copy-start.8 = (bf16[512,192]{0,1:T(8,128)(2,1)S(1)}, bf16[512,192]{0,1:T(8,128)(2,1)}, u32[]{:S(2)}) copy-start(bf16[512,192]{0,1:T(8,128)(2,1)} %param.7) | copy-start | bytes 589828
  58.9 92.0 %all-to-all-start.2 = ((bf16[8,256,512]{2,1,0:T(8,128)(2,1)}), bf16[8,256,512]{2,1,0:T(8,128)(2,1)S(1)}, u32[]{:S(2)}, u32[]{:S(2)}) async-start(bf16[8,256,512]{2,1,0:T(8,128)(2,1)} %copy-done), calls=%async_computation.2 | async-start | bytes 4194304 | tf_op jit(solution)/shard_map/all_to_all | solution.py:158
  63.5 87.3 %all-gather.3.cloned.1.call-start = ((), (), s32[]{:S(2)}) async-start(), calls=%async_computation.4 | async-start | bytes 3342336 | tf_op jit(solution)/shard_map/all_gather | solution.py:152
  63.6 29.5 %collective-permute-start = (bf16[192,512]{1,0:T(8,128)(2,1)S(1)}, bf16[192,512]{1,0:T(8,128)(2,1)S(1)}, u32[]{:S(2)}, u32[]{:S(2)}) collective-permute-start(bf16[192,512]{1,0:T(8,128)(2,1)S(1)} %bitcast.15), channel_id=1, source_target_pairs={{0,0},{1,16},{2,64},{3,80},{4,4},{5,20},{6,68},{7,84},{8,8},{9,24}... | collective-permute-start | bytes 589832 | tf_op jit(solution)/shard_map/ppermute | solution.py:151
  93.1 0.7 copy-start.7
  150.9 1.9 %copy-start.1 = (bf16[3072,512]{1,0:T(8,128)(2,1)S(1)}, bf16[3072,512]{1,0:T(8,128)(2,1)}, u32[]{:S(2)}) copy-start(bf16[3072,512]{1,0:T(8,128)(2,1)} %all-gather.3.cloned.1.call-done) | copy-start | bytes 9437188
Sparse Core Ops, SparseCore 0:
  93.9 56.9 all-gather.2

commit v2 on v1

--- a/solution.py
+++ b/solution.py
@@ -126,7 +126,7 @@
                 for y in range(4):
                     for x in range(4):
                         source = flat(za=za, zb=zj // 2, zc=zj % 2, core=core, y=y, x=x)
-                        target = flat(za=za, zb=x // 2, zc=core, core=x % 2, y=y, x=zj)
+                        target = flat(za=za, zb=x // 2, zc=x % 2, core=core, y=y, x=zj)
                         pairs.append((source, target))
     return pairs
 
@@ -149,18 +149,18 @@
     tokens, width = queries.shape
     columns = out_weight.shape[1]
     moved = lax.ppermute(out_weight.T, AXES, weight_moves())
-    weight = lax.all_gather(moved, ("za", "zb", "core"))
-    weight = weight.reshape(GRID["y"], GRID["x"], columns, width)
+    weight = lax.all_gather(moved, CTX)
+    weight = weight.reshape(GRID["y"], GRID["x"], 2 * columns, width)
 
     prefix = earlier_states(block_states(keys, values))
     index = lax.axis_index(CTX).astype(jnp.int32).reshape(1)
-    attended = attend(index, queries, keys, values, prefix, GRID["zc"] * GRID["x"])
-    attended = lax.all_to_all(attended, ("zc", "x"), 0, 0)
-    attended = attended.reshape(GRID["zc"], GRID["x"], tokens, width)
+    attended = attend(index, queries, keys, values, prefix, GRID["x"])
+    attended = lax.all_to_all(attended, "x", 0, 0)
+    attended = attended.reshape(1, GRID["x"], tokens, width)
     partial = project(weight, attended)
-    partial = partial.reshape(GRID["zc"] * GRID["y"], columns, tokens)
-    parts = lax.all_to_all(partial, ("zc", "y"), 0, 0)
-    return finish(parts.reshape(GRID["zc"], GRID["y"], columns, tokens)).T
+    partial = partial.reshape(GRID["y"], 2 * columns, tokens)
+    parts = lax.all_to_all(partial, "y", 0, 0)
+    return finish(parts.reshape(1, GRID["y"], 2 * columns, tokens)).T
 
 
 def solution(mesh):

time: 181 us -> 139 us (0.77)
  waiting for transfers between devices: 93.6 us -> 24.9 us
  blocking collectives: 33.5 us -> 56 us
  local copies, waits for them, and re-layouts: 6.65 us -> 9.03 us
  starting transfers between devices: 26.6 us -> 28.8 us
    all_gather x1, waiting for transfers between devices: 57.1 us -> 12.3 us  [per_device(): weight = lax.all_gather(moved, CTX)]
    ppermute x1, waiting for transfers between devices: 24.9 us -> 0.01 us  [per_device(): moved = lax.ppermute(out_weight.T, AXES, weight_moves())]
    all_to_all x1 -> x2, blocking collectives: 16.1 us -> 33.9 us  [the longest x1 18.4 us: per_device(): attended = lax.all_to_all(attended, 'x', 0, 0)]
    all_to_all x1, starting transfers between devices: 10.2 us -> 20.1 us  [earlier_states(): pieces = lax.all_to_all(state.reshape(8, rows, DH), NEAR, 0, 0)]
    all_to_all x1 -> x0, starting transfers between devices: 4.61 us -> none  [per_device(): attended = lax.all_to_all(attended, ('zc', 'x'), 0, 0)]
    all_gather x1, blocking collectives: 17.5 us -> 22.1 us  [earlier_states(): totals = lax.all_gather(total.astype(BF16), 'za').astype(F32)]
    ppermute x1, starting transfers between devices: 4.64 us -> 1.57 us  [per_device(): moved = lax.ppermute(out_weight.T, AXES, weight_moves())]
    unnamed x18 -> x14, local copies, waits for them, and re-layouts: 5.83 us -> 8.2 us
  transfers between devices with their start and end apart: 5 -> 4, of which waited for: 4 -> 3; matrix products, arithmetic and copies ran while one was open for 0% -> 1% of each run, Pallas kernels for 0% -> 1%
where the time goes in v2:
time: 139 us; the launch traced here: 137 us
  blocking collectives  56 us (40%)
  starting transfers between devices  28.8 us (21%)
  waiting for transfers between devices  24.9 us (18%)
  between operations  13.4 us (10%)
  local copies, waits for them, and re-layouts  9.03 us (6%)
  Pallas kernels  4.16 us (3%)
    all_gather x1, blocking collectives, earlier_states(): totals = lax.all_gather(total.astype(BF16), 'za').astype(F32)  22.1 us
    all_to_all x1, starting transfers between devices, earlier_states(): pieces = lax.all_to_all(state.reshape(8, rows, DH), NEAR, 0, 0)  20.1 us
    all_to_all x1, blocking collectives, per_device(): attended = lax.all_to_all(attended, 'x', 0, 0)  18.4 us
    all_to_all x1, blocking collectives, per_device(): parts = lax.all_to_all(partial, 'y', 0, 0)  15.5 us
    all_gather x1, waiting for transfers between devices, per_device(): weight = lax.all_gather(moved, CTX)  12.3 us
    unnamed x14, local copies, waits for them, and re-layouts  8.2 us
    all_to_all x1, starting transfers between devices, earlier_states(): return lax.all_to_all(prefix, NEAR, 0, 0).reshape(state.shape)  7.09 us
    all_to_all x1, waiting for transfers between devices, earlier_states(): return lax.all_to_all(prefix, NEAR, 0, 0).reshape(state.shape)  6.83 us
  transfers between devices with their start and end apart: 4, of which 3 were waited for; matrix products, arithmetic and copies ran while one was open for 1% of the time, Pallas kernels for 1%

profile of v2, /device:TPU:1, one launch (start us, length us, event | category | flops | bytes accessed | tf_op | source)
XLA Modules:
  0.0 137.1 jit_solution(3206282810734014195)
XLA Ops:
  6.5 0.0 all-gather.3.cloned.1.call-start
  6.5 1.6 %collective-permute-start = (bf16[192,512]{1,0:T(8,128)(2,1)}, bf16[192,512]{1,0:T(8,128)(2,1)S(1)}, u32[]{:S(2)}, u32[]{:S(2)}) collective-permute-start(bf16[192,512]{1,0:T(8,128)(2,1)} %bitcast.15), channel_id=1, source_target_pairs={{0,0},{1,32},{2,64},{3,96},{4,4},{5,36},{6,68},{7,100},{8,8},{9,40... | collective-permute-start | bytes 589832 | tf_op jit(solution)/shard_map/ppermute | solution.py:151
  8.1 0.0 collective-permute-done
  8.1 0.0 copy-start.6
  8.1 0.7 copy-done.6
  8.8 0.0 all-gather.3.cloned.1.call-update
  8.8 0.0 copy-start.1
  8.8 0.9 copy-done.1
  9.8 0.0 copy-start.3
  9.8 0.9 copy-done.3
  10.7 0.9 block_state.1
  11.6 20.1 %all-to-all-start = ((bf16[8,64,128]{2,1,0:T(8,128)(2,1)}), bf16[8,64,128]{2,1,0:T(8,128)(2,1)S(1)}, u32[]{:S(2)}, u32[]{:S(2)}) async-start(bf16[8,64,128]{2,1,0:T(8,128)(2,1)} %bitcast.3), calls=%async_computation | async-start | bytes 262144 | tf_op jit(solution)/shard_map/all_to_all | solution.py:136
  31.8 5.8 %all-to-all-done = bf16[8,64,128]{2,1,0:T(8,128)(2,1)S(1)} async-done(((bf16[8,64,128]{2,1,0:T(8,128)(2,1)}), bf16[8,64,128]{2,1,0:T(8,128)(2,1)S(1)}, u32[]{:S(2)}, u32[]{:S(2)}) %all-to-all-start) | async-done | bytes 131104 | tf_op jit(solution)/shard_map/all_to_all | solution.py:136
  37.6 22.1 %all_gather.12 = bf16[4,64,128]{2,1,0:T(8,128)(2,1)S(1)} all-gather(bf16[1,64,128]{2,1,0:T(8,128)(2,1)S(1)} %slice.7), channel_id=1, replica_groups=mesh['za'=4,'zb'=2,'zc'=2,'core'=2,'y'=4,'x'=4] {'za'}, dimensions={0}, use_global_device_ids=true | all-gather | bytes 81920 | tf_op jit(solution)/shard_map/all_gather | solution.py:141
  59.7 0.1 select_reduce_fusion
  59.8 0.7 fusion.3
  60.5 7.1 %all-to-all-start.1 = ((bf16[8,64,128]{2,1,0:T(8,128)(2,1)}), bf16[8,64,128]{2,1,0:T(8,128)(2,1)S(1)}, u32[]{:S(2)}, u32[]{:S(2)}) async-start(bf16[8,64,128]{2,1,0:T(8,128)(2,1)} %fusion.3), calls=%async_computation.1 | async-start | bytes 262144 | tf_op jit(solution)/shard_map/all_to_all | solution.py:145
  67.6 6.8 %all-to-all-done.1 = bf16[8,64,128]{2,1,0:T(8,128)(2,1)S(1)} async-done(((bf16[8,64,128]{2,1,0:T(8,128)(2,1)}), bf16[8,64,128]{2,1,0:T(8,128)(2,1)S(1)}, u32[]{:S(2)}, u32[]{:S(2)}) %all-to-all-start.1) | async-done | bytes 131104 | tf_op jit(solution)/shard_map/all_to_all | solution.py:145
  74.4 0.0 copy-start.2
  74.4 0.9 copy-done.2
  75.3 0.0 copy-start.4
  75.3 0.9 copy-done.4
  76.3 0.0 copy-start.5
  76.3 0.9 copy-done.5
  77.2 0.7 attend.1
  78.0 18.4 %all_to_all.20 = bf16[4,256,512]{2,1,0:T(8,128)(2,1)S(1)} all-to-all(bf16[4,256,512]{2,1,0:T(8,128)(2,1)S(1)} %attend.1), channel_id=1, replica_groups=mesh['za'=4,'zb'=2,'zc'=2,'core'=2,'y'=4,'x'=4] {'x'}, dimensions={0} | all-to-all | bytes 2097152 | tf_op jit(solution)/shard_map/all_to_all | solution.py:158
  96.4 12.3 %all-gather.3.cloned.1.call-done = bf16[6144,512]{1,0:T(8,128)(2,1)} async-done(((bf16[192,512]{1,0:T(8,128)(2,1)}), bf16[6144,512]{1,0:T(8,128)(2,1)}) %all-gather.3.cloned.1.call-update) | async-done | bytes 6291472 | tf_op jit(solution)/shard_map/all_gather | solution.py:152
  108.7 0.0 copy-start
  108.7 2.8 %copy-done = bf16[6144,512]{1,0:T(8,128)(2,1)S(1)} copy-done((bf16[6144,512]{1,0:T(8,128)(2,1)S(1)}, bf16[6144,512]{1,0:T(8,128)(2,1)}, u32[]{:S(2)}) %copy-start) | copy-done | bytes 6291480
  111.5 2.4 %project.1 = bf16[1,4,384,256]{3,2,1,0:T(8,128)(2,1)S(1)} custom-call(bf16[4,4,384,512]{3,2,1,0:T(8,128)(2,1)S(1)} %bitcast.9, bf16[1,4,256,512]{3,2,1,0:T(8,128)(2,1)S(1)} %bitcast.10), custom_call_target="tpu_custom_call" | custom-call | tf_op jit(solution)/shard_map/project/pallas_call | solution.py:81
  113.9 15.5 %all_to_all.21 = bf16[4,384,256]{2,1,0:T(8,128)(2,1)S(1)} all-to-all(bf16[4,384,256]{2,1,0:T(8,128)(2,1)S(1)} %bitcast.12), channel_id=1, replica_groups=mesh['za'=4,'zb'=2,'zc'=2,'core'=2,'y'=4,'x'=4] {'y'}, dimensions={0} | all-to-all | bytes 1572864 | tf_op jit(solution)/shard_map/all_to_all | solution.py:162
  129.4 0.1 finish.1
  129.5 0.8 copy.6
  (3 shorter events, 0.0 us)
Async XLA Ops:
  6.5 102.2 %all-gather.3.cloned.1.call-start = ((), (), s32[]{:S(2)}) async-start(), calls=%async_computation.4 | async-start | bytes 6488064 | tf_op jit(solution)/shard_map/all_gather | solution.py:152
  6.5 1.6 %collective-permute-start = (bf16[192,512]{1,0:T(8,128)(2,1)}, bf16[192,512]{1,0:T(8,128)(2,1)S(1)}, u32[]{:S(2)}, u32[]{:S(2)}) collective-permute-start(bf16[192,512]{1,0:T(8,128)(2,1)} %bitcast.15), channel_id=1, source_target_pairs={{0,0},{1,32},{2,64},{3,96},{4,4},{5,36},{6,68},{7,100},{8,8},{9,40... | collective-permute-start | bytes 589832 | tf_op jit(solution)/shard_map/ppermute | solution.py:151
  8.1 0.7 copy-start.6
  8.8 1.0 copy-start.1
  9.8 0.9 copy-start.3
  11.6 25.9 %all-to-all-start = ((bf16[8,64,128]{2,1,0:T(8,128)(2,1)}), bf16[8,64,128]{2,1,0:T(8,128)(2,1)S(1)}, u32[]{:S(2)}, u32[]{:S(2)}) async-start(bf16[8,64,128]{2,1,0:T(8,128)(2,1)} %bitcast.3), calls=%async_computation | async-start | bytes 262144 | tf_op jit(solution)/shard_map/all_to_all | solution.py:136
  60.5 13.9 %all-to-all-start.1 = ((bf16[8,64,128]{2,1,0:T(8,128)(2,1)}), bf16[8,64,128]{2,1,0:T(8,128)(2,1)S(1)}, u32[]{:S(2)}, u32[]{:S(2)}) async-start(bf16[8,64,128]{2,1,0:T(8,128)(2,1)} %fusion.3), calls=%async_computation.1 | async-start | bytes 262144 | tf_op jit(solution)/shard_map/all_to_all | solution.py:145
  74.4 1.0 copy-start.2
  75.3 0.9 copy-start.4
  76.3 0.9 copy-start.5
  108.7 2.8 %copy-start = (bf16[6144,512]{1,0:T(8,128)(2,1)S(1)}, bf16[6144,512]{1,0:T(8,128)(2,1)}, u32[]{:S(2)}) copy-start(bf16[6144,512]{1,0:T(8,128)(2,1)} %all-gather.3.cloned.1.call-done) | copy-start | bytes 18874372
Sparse Core Ops, SparseCore 0:
  9.5 99.1 all-gather.2

commit v3 on v2

v3 whole, which is shorter than its diff:
```python
import functools

import jax
import jax.numpy as jnp
from jax import lax
from jax.experimental import pallas as pl
from jax.experimental.pallas import tpu as pltpu
from jax.sharding import Mesh
from jax.sharding import PartitionSpec as P

DH = 128
BF16 = jnp.bfloat16
F32 = jnp.float32
GRID = {"za": 4, "zb": 2, "zc": 2, "core": 2, "y": 4, "x": 4}
AXES = tuple(GRID)
CTX = ("za", "zb", "zc", "core")
HEAD = ("y", "x")
NEAR = ("zb", "zc", "core")
VMEM = pltpu.CompilerParams(vmem_limit_bytes=32 * 1024 * 1024)


def dot(a, b, dims):
    return lax.dot_general(a, b, (dims, ((), ())), preferred_element_type=F32)


def state_kernel(k_ref, v_ref, out_ref):
    for h in range(k_ref.shape[1] // DH):
        cols = pl.ds(h * DH, DH)
        out_ref[cols, :] = dot(k_ref[:, cols], v_ref[:, cols], ((0,), (0,))).astype(BF16)


def block_states(k, v):
    return pl.pallas_call(
        state_kernel,
        out_shape=jax.ShapeDtypeStruct((k.shape[1], DH), BF16),
        compiler_params=VMEM,
        name="block_state",
    )(k, v)


def attend_kernel(index_ref, q_ref, k_ref, v_ref, prefix_ref, out_ref):
    rows = q_ref.shape[0]
    causal = lax.broadcasted_iota(jnp.int32, (rows, rows), 0) >= lax.broadcasted_iota(
        jnp.int32, (rows, rows), 1
    )
    position = index_ref[0] * rows + lax.broadcasted_iota(jnp.int32, (rows, DH), 0)
    scale = jnp.sqrt(DH * (position.astype(F32) + 1.0))
    for h in range(q_ref.shape[1] // DH):
        cols = pl.ds(h * DH, DH)
        q = q_ref[:, cols]
        scores = jnp.where(causal, dot(q, k_ref[:, cols], ((1,), (1,))), 0.0).astype(BF16)
        both = dot(scores, v_ref[:, cols], ((1,), (0,))) + dot(q, prefix_ref[cols, :], ((1,), (0,)))
        attended = (both / scale).T.astype(BF16)
        for copy in range(out_ref.shape[0]):
            out_ref[copy, cols, :] = attended


def attend(index, q, k, v, prefix, copies):
    whole = pl.BlockSpec(memory_space=pltpu.VMEM)
    return pl.pallas_call(
        attend_kernel,
        out_shape=jax.ShapeDtypeStruct((copies, q.shape[1], q.shape[0]), BF16),
        in_specs=[pl.BlockSpec(memory_space=pltpu.SMEM)] + [whole] * 4,
        out_specs=whole,
        compiler_params=VMEM,
        name="attend",
    )(index, q, k, v, prefix)


def project_kernel(w_ref, a_ref, out_ref):
    shards, groups, columns, width = w_ref.shape
    together = 8
    rows = together * columns
    for i in range(0, shards, together):
        total = dot(w_ref[i : i + together, 0].reshape(rows, width), a_ref[0], ((1,), (0,)))
        for g in range(1, groups):
            part = w_ref[i : i + together, g].reshape(rows, width)
            total += dot(part, a_ref[g], ((1,), (0,)))
        out_ref[pl.ds(i * columns, rows), :] = total.astype(BF16)


def project(weight, attended):
    shards, groups, columns, width = weight.shape
    return pl.pallas_call(
        project_kernel,
        out_shape=jax.ShapeDtypeStruct((shards * columns, attended.shape[2]), BF16),
        compiler_params=VMEM,
        name="project",
    )(weight, attended)


def finish_kernel(parts_ref, out_ref):
    for half in range(parts_ref.shape[2]):
        for x in range(parts_ref.shape[1]):
            total = parts_ref[0, x, half].astype(F32)
            for y in range(1, parts_ref.shape[0]):
                total += parts_ref[y, x, half].astype(F32)
            columns = total.shape[0]
            place = (half * parts_ref.shape[1] + x) * columns
            out_ref[pl.ds(place, columns), :] = total


def turn_kernel(parts_ref, out_ref, total_ref):
    finish_kernel(parts_ref, total_ref)
    out_ref[...] = total_ref[...].T.astype(BF16)


def finish(parts):
    _, x, halves, columns, tokens = parts.shape
    total = x * halves * columns
    return pl.pallas_call(
        turn_kernel,
        out_shape=jax.ShapeDtypeStruct((tokens, total), BF16),
        scratch_shapes=[pltpu.VMEM((total, tokens), F32)],
        compiler_params=VMEM,
        name="finish",
    )(parts)


def earlier_states(state):
    rows = state.shape[0] // 8
    pieces = lax.all_to_all(state.reshape(8, rows, DH), NEAR, 0, 0)
    pieces = pieces.astype(F32)
    running = jnp.cumsum(pieces, axis=0)
    total = running[-1]
    before = running - pieces
    totals = lax.all_gather(total.astype(BF16), "za").astype(F32)
    reached = jnp.arange(GRID["za"])[:, None, None] < lax.axis_index("za")
    carried = jnp.sum(jnp.where(reached, totals, 0.0), axis=0)
    prefix = (before + carried[None]).astype(BF16)
    return lax.all_to_all(prefix, NEAR, 0, 0).reshape(state.shape)


def per_device(queries, keys, values, out_weight):
    tokens, width = queries.shape
    groups = GRID["x"]
    columns = out_weight.shape[1] // groups
    weight = lax.all_to_all(out_weight.T.reshape(groups, columns, width), "x", 0, 0)
    weight = lax.all_gather(weight, CTX)

    states = block_states(keys, values)
    index = lax.axis_index(CTX).astype(jnp.int32).reshape(1)

    def gathered(states):
        prefix = earlier_states(states)
        attended = attend(index, queries, keys, values, prefix, groups)
        return lax.all_to_all(attended, "x", 0, 0)

    def nothing(states):
        return jnp.zeros((groups, width, tokens), BF16)

    attended = lax.cond(lax.axis_index(CTX) < 64, gathered, nothing, states)
    partial = project(weight, attended)
    owners = GRID["y"] * GRID["x"]
    parts = lax.all_to_all(partial.reshape(owners, 2 * columns, tokens), HEAD, 0, 0)
    return finish(parts.reshape(GRID["y"], GRID["x"], 2, columns, tokens))


def solution(mesh):
    grid = Mesh(mesh.devices.reshape(tuple(GRID.values())), AXES)
    spec = P(CTX, HEAD)
    return jax.shard_map(
        per_device,
        mesh=grid,
        in_specs=(spec, spec, spec, P(HEAD, CTX)),
        out_specs=spec,
        check_vma=False,
    )
```

time: 139 us -> 134 us (0.964)
  blocking collectives: 56 us -> 77.3 us
  starting transfers between devices: 28.8 us -> 10.4 us
  local copies, waits for them, and re-layouts: 9.03 us -> 2.79 us
  Pallas kernels: 4.16 us -> 6.45 us
  waiting for transfers between devices: 24.9 us -> 22.8 us
    all_to_all x2 -> x4, blocking collectives: 33.9 us -> 59.2 us  [the longest x1 21.1 us: per_device(): lax.all_to_all(partial.reshape(owners, 2 * columns, tokens), HEAD, 0, 0)]
    all_to_all x1, starting transfers between devices: 20.1 us -> 10.4 us  [earlier_states(): pieces = lax.all_to_all(state.reshape(8, rows, DH), NEAR, 0, 0)]
    all_to_all x1 -> x0, starting transfers between devices: 7.09 us -> none  [earlier_states(): return lax.all_to_all(prefix, NEAR, 0, 0).reshape(state.shape)]
    all_to_all x1 -> x0, waiting for transfers between devices: 6.83 us -> none  [earlier_states(): return lax.all_to_all(prefix, NEAR, 0, 0).reshape(state.shape)]
    unnamed x14 -> x2, local copies, waits for them, and re-layouts: 8.2 us -> 2.78 us
    all_gather x1, waiting for transfers between devices: 12.3 us -> 16.9 us  [per_device(): weight = lax.all_gather(weight, CTX)]
    all_gather x1, blocking collectives: 22.1 us -> 18.2 us  [earlier_states(): totals = lax.all_gather(total.astype(BF16), 'za').astype(F32)]
    ppermute x1 -> x0, starting transfers between devices: 1.57 us -> none  [per_device(): moved = lax.ppermute(out_weight.T, AXES, weight_moves())]
  transfers between devices with their start and end apart: 4 -> 2, of which waited for: 3 -> 2; matrix products, arithmetic and copies ran while one was open for 1% -> 0% of each run, Pallas kernels for 1% -> 3%
where the time goes in v3:
time: 134 us; the launch traced here: 133 us
  blocking collectives  77.3 us (58%)
  waiting for transfers between devices  22.8 us (17%)
  between operations  13.4 us (10%)
  starting transfers between devices  10.4 us (8%)
  Pallas kernels  6.45 us (5%)
  local copies, waits for them, and re-layouts  2.79 us (2%)
    all_to_all x1, blocking collectives, per_device(): lax.all_to_all(partial.reshape(owners, 2 * columns, tokens), HEAD, 0, 0)  21.1 us
    all_gather x1, blocking collectives, earlier_states(): totals = lax.all_gather(total.astype(BF16), 'za').astype(F32)  18.2 us
    all_gather x1, waiting for transfers between devices, per_device(): weight = lax.all_gather(weight, CTX)  16.9 us
    all_to_all x1, blocking collectives, gathered(): return lax.all_to_all(attended, 'x', 0, 0)  15.4 us
    all_to_all x1, blocking collectives, earlier_states(): return lax.all_to_all(prefix, NEAR, 0, 0).reshape(state.shape)  12.5 us
    all_to_all x1, starting transfers between devices, earlier_states(): pieces = lax.all_to_all(state.reshape(8, rows, DH), NEAR, 0, 0)  10.4 us
    all_to_all x1, blocking collectives, per_device(): lax.all_to_all(out_weight.T.reshape(groups, columns, width), 'x', 0, 0)  10.1 us
    all_to_all x1, waiting for transfers between devices, earlier_states(): pieces = lax.all_to_all(state.reshape(8, rows, DH), NEAR, 0, 0)  5.84 us
  transfers between devices with their start and end apart: 2, of which 2 were waited for; matrix products, arithmetic and copies ran while one was open for 0% of the time, Pallas kernels for 3%

profile of v3, /device:TPU:1, one launch (start us, length us, event | category | flops | bytes accessed | tf_op | source)
XLA Modules:
  0.0 133.3 jit_solution(10477152460788432965)
XLA Ops:
  6.5 0.0 all-gather.3.cloned.1.call-start
  6.5 10.1 %all_to_all.24 = bf16[4,48,512]{2,1,0:T(8,128)(2,1)} all-to-all(bf16[4,48,512]{2,1,0:T(8,128)(2,1)} %bitcast.13), channel_id=1, replica_groups=mesh['za'=4,'zb'=2,'zc'=2,'core'=2,'y'=4,'x'=4] {'x'}, dimensions={0} | all-to-all | bytes 393216 | tf_op jit(solution)/shard_map/all_to_all | solution.py:138
  16.7 0.0 all-gather.3.cloned.1.call-update
  16.7 2.0 %block_state.1 = bf16[512,128]{1,0:T(8,128)(2,1)} custom-call(bf16[256,512]{1,0:T(8,128)(2,1)} %k_ref.1, bf16[256,512]{1,0:T(8,128)(2,1)} %v_ref.1), custom_call_target="tpu_custom_call" | custom-call | tf_op jit(solution)/shard_map/block_state/pallas_call | solution.py:33
  18.7 64.4 %conditional.1 = (bf16[4,512,256]{2,1,0:T(8,128)(2,1)S(1)}) conditional(s32[]{:T(128)} %convert_element_type.14, () %tuple.11, (s32[]{:T(128)}, bf16[512,128]{1,0:T(8,128)(2,1)}, bf16[256,512]{1,0:T(8,128)(2,1)}, bf16[256,512]{1,0:T(8,128)(2,1)}, bf16[256,512]{1,0:T(8,128)(2,1)}) %tuple.12), branch_computations={%region_0.0_spmd, %region_1.4_spmd} | conditional | flops 876551 | bytes 3915860 | solution.py:152
  18.7 10.4 %all-to-all-start = ((bf16[8,64,128]{2,1,0:T(8,128)(2,1)}), bf16[8,64,128]{2,1,0:T(8,128)(2,1)S(1)}, u32[]{:S(2)}, u32[]{:S(2)}) async-start(bf16[8,64,128]{2,1,0:T(8,128)(2,1)} %bitcast.1), calls=%async_computation | async-start | bytes 262144 | tf_op jit(solution)/shard_map/cond/branch_1_fun/all_to_all | solution.py:122
  29.1 5.8 %all-to-all-done = bf16[8,64,128]{2,1,0:T(8,128)(2,1)S(1)} async-done(((bf16[8,64,128]{2,1,0:T(8,128)(2,1)}), bf16[8,64,128]{2,1,0:T(8,128)(2,1)S(1)}, u32[]{:S(2)}, u32[]{:S(2)}) %all-to-all-start) | async-done | bytes 131104 | tf_op jit(solution)/shard_map/cond/branch_1_fun/all_to_all | solution.py:122
  34.9 18.2 %all_gather.2 = bf16[4,64,128]{2,1,0:T(8,128)(2,1)S(1)} all-gather(bf16[1,64,128]{2,1,0:T(8,128)(2,1)S(1)} %slice.6), channel_id=1, replica_groups=mesh['za'=4,'zb'=2,'zc'=2,'core'=2,'y'=4,'x'=4] {'za'}, dimensions={0}, use_global_device_ids=true | all-gather | bytes 81920 | tf_op jit(solution)/shard_map/cond/branch_1_fun/all_gather | solution.py:127
  53.1 0.1 select_reduce_fusion
  53.2 12.5 %all_to_all.22 = bf16[8,64,128]{2,1,0:T(8,128)(2,1)S(1)} all-to-all(bf16[8,64,128]{2,1,0:T(8,128)(2,1)S(1)} %fusion.3), channel_id=1, replica_groups=mesh['za'=4,'zb'=2,'zc'=2,'core'=2,'y'=4,'x'=4] {'zb','zc','core'}, dimensions={0} | all-to-all | bytes 262144 | tf_op jit(solution)/shard_map/cond/branch_1_fun/all_to_all | solution.py:131
  65.8 1.9 %attend.1 = bf16[4,512,256]{2,1,0:T(8,128)(2,1)S(1)} custom-call(s32[1]{0:T(128)} %bitcast.index_ref, bf16[256,512]{1,0:T(8,128)(2,1)} %get-tuple-element.25.q_ref, bf16[256,512]{1,0:T(8,128)(2,1)} %get-tuple-element.21.k_ref, bf16[256,512]{1,0:T(8,128)(2,1)} %get-tuple-element.22.v_ref, bf16[512,128]{1,0:T(8,128)(2,1)S(1)} %bitcast.12), custom_call_target="tpu_custom_call" | custom-call | tf_op jit(solution)/shard_map/cond/branch_1_fun/attend/pallas_call | solution.py:60
  67.6 15.4 %all_to_all.23 = bf16[4,512,256]{2,1,0:T(8,128)(2,1)S(1)} all-to-all(bf16[4,512,256]{2,1,0:T(8,128)(2,1)S(1)} %attend.1), channel_id=1, replica_groups=mesh['za'=4,'zb'=2,'zc'=2,'core'=2,'y'=4,'x'=4] {'x'}, dimensions={0} | all-to-all | bytes 2097152 | tf_op jit(solution)/shard_map/cond/branch_1_fun/all_to_all | solution.py:147
  83.0 16.9 %all-gather.3.cloned.1.call-done = bf16[128,48,512]{2,1,0:T(8,128)(2,1)} async-done(((bf16[4,48,512]{2,1,0:T(8,128)(2,1)}), bf16[128,48,512]{2,1,0:T(8,128)(2,1)}) %all-gather.3.cloned.1.call-update) | async-done | bytes 6291472 | tf_op jit(solution)/shard_map/all_gather | solution.py:139
  100.0 0.0 copy-start
  100.0 2.8 %copy-done = bf16[128,48,512]{2,1,0:T(8,128)(2,1)S(1)} copy-done((bf16[128,48,512]{2,1,0:T(8,128)(2,1)S(1)}, bf16[128,48,512]{2,1,0:T(8,128)(2,1)}, u32[]{:S(2)}) %copy-start) | copy-done | bytes 6291480
  102.8 1.8 %project.1 = bf16[1536,256]{1,0:T(8,128)(2,1)S(1)} custom-call(bf16[32,4,48,512]{3,2,1,0:T(8,128)(2,1)S(1)} %bitcast.9, bf16[4,512,256]{2,1,0:T(8,128)(2,1)S(1)} %get-tuple-element.26.a_ref), custom_call_target="tpu_custom_call" | custom-call | tf_op jit(solution)/shard_map/project/pallas_call | solution.py:84
  104.5 21.1 %all_to_all.25 = bf16[16,96,256]{2,1,0:T(8,128)(2,1)S(1)} all-to-all(bf16[16,96,256]{2,1,0:T(8,128)(2,1)S(1)} %bitcast.11), channel_id=1, replica_groups=mesh['za'=4,'zb'=2,'zc'=2,'core'=2,'y'=4,'x'=4] {'y','x'}, dimensions={0} | all-to-all | bytes 1572864 | tf_op jit(solution)/shard_map/all_to_all | solution.py:155
  125.6 0.8 finish.1
  (4 shorter events, 0.1 us)
Async XLA Ops:
  6.5 93.4 %all-gather.3.cloned.1.call-start = ((), (), s32[]{:S(2)}) async-start(), calls=%async_computation.5 | async-start | bytes 6488064 | tf_op jit(solution)/shard_map/all_gather | solution.py:139
  18.7 16.2 %all-to-all-start = ((bf16[8,64,128]{2,1,0:T(8,128)(2,1)}), bf16[8,64,128]{2,1,0:T(8,128)(2,1)S(1)}, u32[]{:S(2)}, u32[]{:S(2)}) async-start(bf16[8,64,128]{2,1,0:T(8,128)(2,1)} %bitcast.1), calls=%async_computation | async-start | bytes 262144 | tf_op jit(solution)/shard_map/cond/branch_1_fun/all_to_all | solution.py:122
  100.0 2.8 %copy-start = (bf16[128,48,512]{2,1,0:T(8,128)(2,1)S(1)}, bf16[128,48,512]{2,1,0:T(8,128)(2,1)}, u32[]{:S(2)}) copy-start(bf16[128,48,512]{2,1,0:T(8,128)(2,1)} %all-gather.3.cloned.1.call-done) | copy-start | bytes 18874372
Sparse Core Ops, SparseCore 0:
  16.8 83.1 all-gather.2

commit v4 on v3

--- a/solution.py
+++ b/solution.py
@@ -67,36 +67,41 @@
     )(index, q, k, v, prefix)
 
 
-def project_kernel(w_ref, a_ref, out_ref):
+def project_kernel(core_ref, w_ref, own_ref, other_ref, out_ref):
     shards, groups, columns, width = w_ref.shape
     together = 8
     rows = together * columns
-    for i in range(0, shards, together):
-        total = dot(w_ref[i : i + together, 0].reshape(rows, width), a_ref[0], ((1,), (0,)))
-        for g in range(1, groups):
-            part = w_ref[i : i + together, g].reshape(rows, width)
-            total += dot(part, a_ref[g], ((1,), (0,)))
-        out_ref[pl.ds(i * columns, rows), :] = total.astype(BF16)
+    for which, a_ref in enumerate((own_ref, other_ref)):
+        place = lax.bitwise_xor(core_ref[0], which)
+        for i in range(0, shards, together):
+            total = dot(w_ref[i : i + together, 0].reshape(rows, width), a_ref[0], ((1,), (0,)))
+            for g in range(1, groups):
+                part = w_ref[i : i + together, g].reshape(rows, width)
+                total += dot(part, a_ref[g], ((1,), (0,)))
+            out_ref[place, i : i + together] = total.astype(BF16).reshape(together, columns, -1)
 
 
-def project(weight, attended):
-    shards, groups, columns, width = weight.shape
+def project(core, weight, own, other):
+    shards, _, columns, _ = weight.shape
+    vmem = pl.BlockSpec(memory_space=pltpu.VMEM)
     return pl.pallas_call(
         project_kernel,
-        out_shape=jax.ShapeDtypeStruct((shards * columns, attended.shape[2]), BF16),
+        out_shape=jax.ShapeDtypeStruct((2, shards, columns, own.shape[2]), BF16),
+        in_specs=[pl.BlockSpec(memory_space=pltpu.SMEM)] + [vmem] * 3,
+        out_specs=vmem,
         compiler_params=VMEM,
         name="project",
-    )(weight, attended)
+    )(core, weight, own, other)
 
 
 def finish_kernel(parts_ref, out_ref):
-    for half in range(parts_ref.shape[2]):
-        for x in range(parts_ref.shape[1]):
-            total = parts_ref[0, x, half].astype(F32)
-            for y in range(1, parts_ref.shape[0]):
-                total += parts_ref[y, x, half].astype(F32)
+    for half in range(parts_ref.shape[0]):
+        for x in range(parts_ref.shape[2]):
+            total = parts_ref[half, 0, x].astype(F32)
+            for y in range(1, parts_ref.shape[1]):
+                total += parts_ref[half, y, x].astype(F32)
             columns = total.shape[0]
-            place = (half * parts_ref.shape[1] + x) * columns
+            place = (half * parts_ref.shape[2] + x) * columns
             out_ref[pl.ds(place, columns), :] = total
 
 
@@ -106,7 +111,7 @@
 
 
 def finish(parts):
-    _, x, halves, columns, tokens = parts.shape
+    halves, _, x, columns, tokens = parts.shape
     total = x * halves * columns
     return pl.pallas_call(
         turn_kernel,
@@ -136,7 +141,7 @@
     groups = GRID["x"]
     columns = out_weight.shape[1] // groups
     weight = lax.all_to_all(out_weight.T.reshape(groups, columns, width), "x", 0, 0)
-    weight = lax.all_gather(weight, CTX)
+    weight = lax.all_gather(weight, ("za", "zb", "zc"))
 
     states = block_states(keys, values)
     index = lax.axis_index(CTX).astype(jnp.int32).reshape(1)
@@ -150,10 +155,11 @@
         return jnp.zeros((groups, width, tokens), BF16)
 
     attended = lax.cond(lax.axis_index(CTX) < 64, gathered, nothing, states)
-    partial = project(weight, attended)
-    owners = GRID["y"] * GRID["x"]
-    parts = lax.all_to_all(partial.reshape(owners, 2 * columns, tokens), HEAD, 0, 0)
-    return finish(parts.reshape(GRID["y"], GRID["x"], 2, columns, tokens))
+    other = lax.ppermute(attended, "core", [(0, 1), (1, 0)])
+    core = lax.axis_index("core").astype(jnp.int32).reshape(1)
+    partial = project(core, weight, attended, other)
+    parts = lax.all_to_all(partial.reshape(32, columns, tokens), ("core",) + HEAD, 0, 0)
+    return finish(parts.reshape(2, GRID["y"], GRID["x"], columns, tokens))
 
 
 def solution(mesh):

time: 134 us -> 133 us (level)
  waiting for transfers between devices: 22.8 us -> 8.7 us
  blocking collectives: 77.3 us -> 86.6 us
  starting transfers between devices: 10.4 us -> 14.9 us
    all_gather x1, waiting for transfers between devices: 16.9 us -> 0.58 us  [per_device(): weight = lax.all_gather(weight, ('za', 'zb', 'zc'))]
    all_to_all x1, blocking collectives: 21.1 us -> 29.5 us  [per_device(): lax.all_to_all(partial.reshape(32, columns, tokens), ('core',) + HEAD, 0, 0)]
    ppermute x0 -> x1, starting transfers between devices: none -> 4.49 us  [per_device(): other = lax.ppermute(attended, 'core', [(0, 1), (1, 0)])]
    ppermute x0 -> x1, waiting for transfers between devices: none -> 2.26 us  [per_device(): other = lax.ppermute(attended, 'core', [(0, 1), (1, 0)])]
  transfers between devices with their start and end apart: 2 -> 3, of which waited for: 2 -> 3; matrix products, arithmetic and copies ran while one was open for 0% -> 0% of each run, Pallas kernels for 3% -> 3%
where the time goes in v4:
time: 133 us; the launch traced here: 132 us
  blocking collectives  86.6 us (65%)
  starting transfers between devices  14.9 us (11%)
  between operations  13.4 us (10%)
  waiting for transfers between devices  8.7 us (7%)
  Pallas kernels  6.46 us (5%)
  local copies, waits for them, and re-layouts  1.89 us (1%)
    all_to_all x1, blocking collectives, per_device(): lax.all_to_all(partial.reshape(32, columns, tokens), ('core',) + HEAD, 0, 0)  29.5 us
    all_gather x1, blocking collectives, earlier_states(): totals = lax.all_gather(total.astype(BF16), 'za').astype(F32)  18.2 us
    all_to_all x1, blocking collectives, gathered(): return lax.all_to_all(attended, 'x', 0, 0)  16.3 us
    all_to_all x1, blocking collectives, earlier_states(): return lax.all_to_all(prefix, NEAR, 0, 0).reshape(state.shape)  12.4 us
    all_to_all x1, starting transfers between devices, earlier_states(): pieces = lax.all_to_all(state.reshape(8, rows, DH), NEAR, 0, 0)  10.4 us
    all_to_all x1, blocking collectives, per_device(): lax.all_to_all(out_weight.T.reshape(groups, columns, width), 'x', 0, 0)  10.1 us
    all_to_all x1, waiting for transfers between devices, earlier_states(): pieces = lax.all_to_all(state.reshape(8, rows, DH), NEAR, 0, 0)  5.84 us
    ppermute x1, starting transfers between devices, per_device(): other = lax.ppermute(attended, 'core', [(0, 1), (1, 0)])  4.49 us
  transfers between devices with their start and end apart: 3, of which 3 were waited for; matrix products, arithmetic and copies ran while one was open for 0% of the time, Pallas kernels for 3%

profile of v4, /device:TPU:1, one launch (start us, length us, event | category | flops | bytes accessed | tf_op | source)
XLA Modules:
  0.0 132.1 jit_solution(16014065600763043237)
XLA Ops:
  6.5 0.0 all-gather.3.cloned.1.call-start
  6.5 10.1 %all_to_all.24 = bf16[4,48,512]{2,1,0:T(8,128)(2,1)} all-to-all(bf16[4,48,512]{2,1,0:T(8,128)(2,1)} %bitcast.14), channel_id=1, replica_groups=mesh['za'=4,'zb'=2,'zc'=2,'core'=2,'y'=4,'x'=4] {'x'}, dimensions={0} | all-to-all | bytes 393216 | tf_op jit(solution)/shard_map/all_to_all | solution.py:143
  16.7 0.0 all-gather.3.cloned.1.call-update
  16.7 2.0 %block_state.1 = bf16[512,128]{1,0:T(8,128)(2,1)} custom-call(bf16[256,512]{1,0:T(8,128)(2,1)} %k_ref.1, bf16[256,512]{1,0:T(8,128)(2,1)} %v_ref.1), custom_call_target="tpu_custom_call" | custom-call | tf_op jit(solution)/shard_map/block_state/pallas_call | solution.py:33
  18.7 65.2 %conditional.1 = (bf16[4,512,256]{2,1,0:T(8,128)(2,1)S(1)}) conditional(s32[]{:T(128)} %convert_element_type.14, () %tuple.11, (s32[]{:T(128)}, bf16[512,128]{1,0:T(8,128)(2,1)}, bf16[256,512]{1,0:T(8,128)(2,1)}, bf16[256,512]{1,0:T(8,128)(2,1)}, bf16[256,512]{1,0:T(8,128)(2,1)}) %tuple.12), branch_computations={%region_0.0_spmd, %region_1.4_spmd} | conditional | flops 876551 | bytes 3915860 | solution.py:157
  18.7 10.4 %all-to-all-start = ((bf16[8,64,128]{2,1,0:T(8,128)(2,1)}), bf16[8,64,128]{2,1,0:T(8,128)(2,1)S(1)}, u32[]{:S(2)}, u32[]{:S(2)}) async-start(bf16[8,64,128]{2,1,0:T(8,128)(2,1)} %bitcast.1), calls=%async_computation | async-start | bytes 262144 | tf_op jit(solution)/shard_map/cond/branch_1_fun/all_to_all | solution.py:127
  29.1 5.8 %all-to-all-done = bf16[8,64,128]{2,1,0:T(8,128)(2,1)S(1)} async-done(((bf16[8,64,128]{2,1,0:T(8,128)(2,1)}), bf16[8,64,128]{2,1,0:T(8,128)(2,1)S(1)}, u32[]{:S(2)}, u32[]{:S(2)}) %all-to-all-start) | async-done | bytes 131104 | tf_op jit(solution)/shard_map/cond/branch_1_fun/all_to_all | solution.py:127
  34.9 18.2 %all_gather.2 = bf16[4,64,128]{2,1,0:T(8,128)(2,1)S(1)} all-gather(bf16[1,64,128]{2,1,0:T(8,128)(2,1)S(1)} %slice.6), channel_id=1, replica_groups=mesh['za'=4,'zb'=2,'zc'=2,'core'=2,'y'=4,'x'=4] {'za'}, dimensions={0}, use_global_device_ids=true | all-gather | bytes 81920 | tf_op jit(solution)/shard_map/cond/branch_1_fun/all_gather | solution.py:132
  53.1 0.1 select_reduce_fusion
  53.3 12.4 %all_to_all.22 = bf16[8,64,128]{2,1,0:T(8,128)(2,1)S(1)} all-to-all(bf16[8,64,128]{2,1,0:T(8,128)(2,1)S(1)} %fusion.3), channel_id=1, replica_groups=mesh['za'=4,'zb'=2,'zc'=2,'core'=2,'y'=4,'x'=4] {'zb','zc','core'}, dimensions={0} | all-to-all | bytes 262144 | tf_op jit(solution)/shard_map/cond/branch_1_fun/all_to_all | solution.py:136
  65.7 1.9 %attend.1 = bf16[4,512,256]{2,1,0:T(8,128)(2,1)S(1)} custom-call(s32[1]{0:T(128)} %bitcast.index_ref, bf16[256,512]{1,0:T(8,128)(2,1)} %get-tuple-element.25.q_ref, bf16[256,512]{1,0:T(8,128)(2,1)} %get-tuple-element.21.k_ref, bf16[256,512]{1,0:T(8,128)(2,1)} %get-tuple-element.22.v_ref, bf16[512,128]{1,0:T(8,128)(2,1)S(1)} %bitcast.13), custom_call_target="tpu_custom_call" | custom-call | tf_op jit(solution)/shard_map/cond/branch_1_fun/attend/pallas_call | solution.py:60
  67.6 16.3 %all_to_all.23 = bf16[4,512,256]{2,1,0:T(8,128)(2,1)S(1)} all-to-all(bf16[4,512,256]{2,1,0:T(8,128)(2,1)S(1)} %attend.1), channel_id=1, replica_groups=mesh['za'=4,'zb'=2,'zc'=2,'core'=2,'y'=4,'x'=4] {'x'}, dimensions={0} | all-to-all | bytes 2097152 | tf_op jit(solution)/shard_map/cond/branch_1_fun/all_to_all | solution.py:152
  83.9 4.5 %collective-permute-start = (bf16[4,512,256]{2,1,0:T(8,128)(2,1)S(1)}, bf16[4,512,256]{2,1,0:T(8,128)(2,1)S(1)}, u32[]{:S(2)}, u32[]{:S(2)}) collective-permute-start(bf16[4,512,256]{2,1,0:T(8,128)(2,1)S(1)} %get-tuple-element.26.own_ref), channel_id=1, source_target_pairs={{0,16},{16,0},{1,17},{17,1},{2,18},{18,2},{3,19},{19,3},{4,20},{20... | collective-permute-start | bytes 3145736 | tf_op jit(solution)/shard_map/ppermute | solution.py:158
  88.4 2.3 %collective-permute-done.other_ref = bf16[4,512,256]{2,1,0:T(8,128)(2,1)S(1)} collective-permute-done((bf16[4,512,256]{2,1,0:T(8,128)(2,1)S(1)}, bf16[4,512,256]{2,1,0:T(8,128)(2,1)S(1)}, u32[]{:S(2)}, u32[]{:S(2)}) %collective-permute-start) | collective-permute-done | bytes 1048608 | tf_op jit(solution)/shard_map/ppermute | solution.py:158
  90.7 0.6 all-gather.3.cloned.1.call-done
  91.2 0.0 copy-start
  91.2 1.9 %copy-done = bf16[64,48,512]{2,1,0:T(8,128)(2,1)S(1)} copy-done((bf16[64,48,512]{2,1,0:T(8,128)(2,1)S(1)}, bf16[64,48,512]{2,1,0:T(8,128)(2,1)}, u32[]{:S(2)}) %copy-start) | copy-done | bytes 3145752
  93.1 1.8 %project.1 = bf16[2,16,48,256]{3,2,1,0:T(8,128)(2,1)S(1)} custom-call(s32[1]{0:T(128)} %bitcast.3.core_ref, bf16[16,4,48,512]{3,2,1,0:T(8,128)(2,1)S(1)} %bitcast.11, bf16[4,512,256]{2,1,0:T(8,128)(2,1)S(1)} %get-tuple-element.26.own_ref, bf16[4,512,256]{2,1,0:T(8,128)(2,1)S(1)} %collective-permute-done.other_ref), custom_call_target="tpu_custom_call" | custom-call | tf_op jit(solution)/shard_map/project/pallas_call | solution.py:87
  94.9 29.5 %all_to_all.25 = bf16[32,48,256]{2,1,0:T(8,128)(2,1)S(1)} all-to-all(bf16[32,48,256]{2,1,0:T(8,128)(2,1)S(1)} %bitcast.10), channel_id=1, replica_groups=mesh['za'=4,'zb'=2,'zc'=2,'core'=2,'y'=4,'x'=4] {'core','y','x'}, dimensions={0} | all-to-all | bytes 1572864 | tf_op jit(solution)/shard_map/all_to_all | solution.py:161
  124.4 0.8 finish.1
  (4 shorter events, 0.1 us)
Async XLA Ops:
  6.5 84.7 %all-gather.3.cloned.1.call-start = ((), (), s32[]{:S(2)}) async-start(), calls=%async_computation.5 | async-start | bytes 3342336 | tf_op jit(solution)/shard_map/all_gather | solution.py:144
  18.7 16.3 %all-to-all-start = ((bf16[8,64,128]{2,1,0:T(8,128)(2,1)}), bf16[8,64,128]{2,1,0:T(8,128)(2,1)S(1)}, u32[]{:S(2)}, u32[]{:S(2)}) async-start(bf16[8,64,128]{2,1,0:T(8,128)(2,1)} %bitcast.1), calls=%async_computation | async-start | bytes 262144 | tf_op jit(solution)/shard_map/cond/branch_1_fun/all_to_all | solution.py:127
  83.9 6.8 %collective-permute-start = (bf16[4,512,256]{2,1,0:T(8,128)(2,1)S(1)}, bf16[4,512,256]{2,1,0:T(8,128)(2,1)S(1)}, u32[]{:S(2)}, u32[]{:S(2)}) collective-permute-start(bf16[4,512,256]{2,1,0:T(8,128)(2,1)S(1)} %get-tuple-element.26.own_ref), channel_id=1, source_target_pairs={{0,16},{16,0},{1,17},{17,1},{2,18},{18,2},{3,19},{19,3},{4,20},{20... | collective-permute-start | bytes 3145736 | tf_op jit(solution)/shard_map/ppermute | solution.py:158
  91.2 1.9 %copy-start = (bf16[64,48,512]{2,1,0:T(8,128)(2,1)S(1)}, bf16[64,48,512]{2,1,0:T(8,128)(2,1)}, u32[]{:S(2)}) copy-start(bf16[64,48,512]{2,1,0:T(8,128)(2,1)} %all-gather.3.cloned.1.call-done) | copy-start | bytes 9437188
Sparse Core Ops, SparseCore 0:
  16.8 74.3 all-gather.2

commit v5 on v4

--- a/solution.py
+++ b/solution.py
@@ -129,7 +129,7 @@
     running = jnp.cumsum(pieces, axis=0)
     total = running[-1]
     before = running - pieces
-    totals = lax.all_gather(total.astype(BF16), "za").astype(F32)
+    totals = lax.all_gather(total, "za")
     reached = jnp.arange(GRID["za"])[:, None, None] < lax.axis_index("za")
     carried = jnp.sum(jnp.where(reached, totals, 0.0), axis=0)
     prefix = (before + carried[None]).astype(BF16)

time: 133 us -> 133 us (level)
  transfers between devices with their start and end apart: 3 -> 3, of which waited for: 3 -> 2; matrix products, arithmetic and copies ran while one was open for 0% -> 0% of each run, Pallas kernels for 3% -> 3%
where the time goes in v5:
time: 133 us; the launch traced here: 132 us
  blocking collectives  87.5 us (66%)
  starting transfers between devices  14.4 us (11%)
  between operations  13.4 us (10%)
  waiting for transfers between devices  8.12 us (6%)
  Pallas kernels  6.45 us (5%)
  local copies, waits for them, and re-layouts  1.89 us (1%)
    all_to_all x1, blocking collectives, per_device(): lax.all_to_all(partial.reshape(32, columns, tokens), ('core',) + HEAD, 0, 0)  28.4 us
    all_gather x1, blocking collectives, earlier_states(): totals = lax.all_gather(total, 'za')  18.7 us
    all_to_all x1, blocking collectives, gathered(): return lax.all_to_all(attended, 'x', 0, 0)  17.2 us
    all_to_all x1, blocking collectives, earlier_states(): return lax.all_to_all(prefix, NEAR, 0, 0).reshape(state.shape)  13 us
    all_to_all x1, starting transfers between devices, earlier_states(): pieces = lax.all_to_all(state.reshape(8, rows, DH), NEAR, 0, 0)  10.4 us
    all_to_all x1, blocking collectives, per_device(): lax.all_to_all(out_weight.T.reshape(groups, columns, width), 'x', 0, 0)  10.1 us
    all_to_all x1, waiting for transfers between devices, earlier_states(): pieces = lax.all_to_all(state.reshape(8, rows, DH), NEAR, 0, 0)  5.84 us
    ppermute x1, starting transfers between devices, per_device(): other = lax.ppermute(attended, 'core', [(0, 1), (1, 0)])  4.03 us
  transfers between devices with their start and end apart: 3, of which 2 were waited for; matrix products, arithmetic and copies ran while one was open for 0% of the time, Pallas kernels for 3%

profile of v5, /device:TPU:1, one launch (start us, length us, event | category | flops | bytes accessed | tf_op | source)
XLA Modules:
  0.0 132.0 jit_solution(8938011765286163960)
XLA Ops:
  6.5 0.0 all-gather.3.cloned.1.call-start
  6.5 10.1 %all_to_all.24 = bf16[4,48,512]{2,1,0:T(8,128)(2,1)} all-to-all(bf16[4,48,512]{2,1,0:T(8,128)(2,1)} %bitcast.14), channel_id=1, replica_groups=mesh['za'=4,'zb'=2,'zc'=2,'core'=2,'y'=4,'x'=4] {'x'}, dimensions={0} | all-to-all | bytes 393216 | tf_op jit(solution)/shard_map/all_to_all | solution.py:143
  16.7 0.0 all-gather.3.cloned.1.call-update
  16.7 2.0 %block_state.1 = bf16[512,128]{1,0:T(8,128)(2,1)} custom-call(bf16[256,512]{1,0:T(8,128)(2,1)} %k_ref.1, bf16[256,512]{1,0:T(8,128)(2,1)} %v_ref.1), custom_call_target="tpu_custom_call" | custom-call | tf_op jit(solution)/shard_map/block_state/pallas_call | solution.py:33
  18.7 67.3 %conditional.1 = (bf16[4,512,256]{2,1,0:T(8,128)(2,1)S(1)}) conditional(s32[]{:T(128)} %convert_element_type.9, () %tuple.11, (s32[]{:T(128)}, bf16[512,128]{1,0:T(8,128)(2,1)}, bf16[256,512]{1,0:T(8,128)(2,1)}, bf16[256,512]{1,0:T(8,128)(2,1)}, bf16[256,512]{1,0:T(8,128)(2,1)}) %tuple.12), branch_computations={%region_0.0_spmd, %region_1.4_spmd} | conditional | flops 843783 | bytes 4096084 | solution.py:157
  18.7 10.4 %all-to-all-start = ((bf16[8,64,128]{2,1,0:T(8,128)(2,1)}), bf16[8,64,128]{2,1,0:T(8,128)(2,1)S(1)}, u32[]{:S(2)}, u32[]{:S(2)}) async-start(bf16[8,64,128]{2,1,0:T(8,128)(2,1)} %bitcast.1), calls=%async_computation | async-start | bytes 262144 | tf_op jit(solution)/shard_map/cond/branch_1_fun/all_to_all | solution.py:127
  29.1 5.8 %all-to-all-done = bf16[8,64,128]{2,1,0:T(8,128)(2,1)S(1)} async-done(((bf16[8,64,128]{2,1,0:T(8,128)(2,1)}), bf16[8,64,128]{2,1,0:T(8,128)(2,1)S(1)}, u32[]{:S(2)}, u32[]{:S(2)}) %all-to-all-start) | async-done | bytes 131104 | tf_op jit(solution)/shard_map/cond/branch_1_fun/all_to_all | solution.py:127
  34.9 18.7 %all_gather.6 = f32[4,64,128]{2,1,0:T(8,128)S(1)} all-gather(f32[1,64,128]{2,1,0:T(8,128)S(1)} %slice.3), channel_id=1, replica_groups=mesh['za'=4,'zb'=2,'zc'=2,'core'=2,'y'=4,'x'=4] {'za'}, dimensions={0}, use_global_device_ids=true | all-gather | bytes 163840 | tf_op jit(solution)/shard_map/cond/branch_1_fun/all_gather | solution.py:132
  53.7 0.1 select_reduce_fusion
  53.8 13.0 %all_to_all.22 = bf16[8,64,128]{2,1,0:T(8,128)(2,1)S(1)} all-to-all(bf16[8,64,128]{2,1,0:T(8,128)(2,1)S(1)} %fusion.3), channel_id=1, replica_groups=mesh['za'=4,'zb'=2,'zc'=2,'core'=2,'y'=4,'x'=4] {'zb','zc','core'}, dimensions={0} | all-to-all | bytes 262144 | tf_op jit(solution)/shard_map/cond/branch_1_fun/all_to_all | solution.py:136
  66.8 1.9 %attend.1 = bf16[4,512,256]{2,1,0:T(8,128)(2,1)S(1)} custom-call(s32[1]{0:T(128)} %bitcast.index_ref, bf16[256,512]{1,0:T(8,128)(2,1)} %get-tuple-element.25.q_ref, bf16[256,512]{1,0:T(8,128)(2,1)} %get-tuple-element.21.k_ref, bf16[256,512]{1,0:T(8,128)(2,1)} %get-tuple-element.22.v_ref, bf16[512,128]{1,0:T(8,128)(2,1)S(1)} %bitcast.13), custom_call_target="tpu_custom_call" | custom-call | tf_op jit(solution)/shard_map/cond/branch_1_fun/attend/pallas_call | solution.py:60
  68.7 17.2 %all_to_all.23 = bf16[4,512,256]{2,1,0:T(8,128)(2,1)S(1)} all-to-all(bf16[4,512,256]{2,1,0:T(8,128)(2,1)S(1)} %attend.1), channel_id=1, replica_groups=mesh['za'=4,'zb'=2,'zc'=2,'core'=2,'y'=4,'x'=4] {'x'}, dimensions={0} | all-to-all | bytes 2097152 | tf_op jit(solution)/shard_map/cond/branch_1_fun/all_to_all | solution.py:152
  85.9 4.0 %collective-permute-start = (bf16[4,512,256]{2,1,0:T(8,128)(2,1)S(1)}, bf16[4,512,256]{2,1,0:T(8,128)(2,1)S(1)}, u32[]{:S(2)}, u32[]{:S(2)}) collective-permute-start(bf16[4,512,256]{2,1,0:T(8,128)(2,1)S(1)} %get-tuple-element.26.own_ref), channel_id=1, source_target_pairs={{0,16},{16,0},{1,17},{17,1},{2,18},{18,2},{3,19},{19,3},{4,20},{20... | collective-permute-start | bytes 3145736 | tf_op jit(solution)/shard_map/ppermute | solution.py:158
  90.0 2.3 %collective-permute-done.other_ref = bf16[4,512,256]{2,1,0:T(8,128)(2,1)S(1)} collective-permute-done((bf16[4,512,256]{2,1,0:T(8,128)(2,1)S(1)}, bf16[4,512,256]{2,1,0:T(8,128)(2,1)S(1)}, u32[]{:S(2)}, u32[]{:S(2)}) %collective-permute-start) | collective-permute-done | bytes 1048608 | tf_op jit(solution)/shard_map/ppermute | solution.py:158
  92.2 0.0 all-gather.3.cloned.1.call-done
  92.2 0.0 copy-start
  92.2 1.9 %copy-done = bf16[64,48,512]{2,1,0:T(8,128)(2,1)S(1)} copy-done((bf16[64,48,512]{2,1,0:T(8,128)(2,1)S(1)}, bf16[64,48,512]{2,1,0:T(8,128)(2,1)}, u32[]{:S(2)}) %copy-start) | copy-done | bytes 3145752
  94.1 1.8 %project.1 = bf16[2,16,48,256]{3,2,1,0:T(8,128)(2,1)S(1)} custom-call(s32[1]{0:T(128)} %bitcast.3.core_ref, bf16[16,4,48,512]{3,2,1,0:T(8,128)(2,1)S(1)} %bitcast.11, bf16[4,512,256]{2,1,0:T(8,128)(2,1)S(1)} %get-tuple-element.26.own_ref, bf16[4,512,256]{2,1,0:T(8,128)(2,1)S(1)} %collective-permute-done.other_ref), custom_call_target="tpu_custom_call" | custom-call | tf_op jit(solution)/shard_map/project/pallas_call | solution.py:87
  95.9 28.4 %all_to_all.25 = bf16[32,48,256]{2,1,0:T(8,128)(2,1)S(1)} all-to-all(bf16[32,48,256]{2,1,0:T(8,128)(2,1)S(1)} %bitcast.10), channel_id=1, replica_groups=mesh['za'=4,'zb'=2,'zc'=2,'core'=2,'y'=4,'x'=4] {'core','y','x'}, dimensions={0} | all-to-all | bytes 1572864 | tf_op jit(solution)/shard_map/all_to_all | solution.py:161
  124.3 0.8 finish.1
  (4 shorter events, 0.1 us)
Async XLA Ops:
  6.5 85.7 %all-gather.3.cloned.1.call-start = ((), (), s32[]{:S(2)}) async-start(), calls=%async_computation.5 | async-start | bytes 3342336 | tf_op jit(solution)/shard_map/all_gather | solution.py:144
  18.7 16.3 %all-to-all-start = ((bf16[8,64,128]{2,1,0:T(8,128)(2,1)}), bf16[8,64,128]{2,1,0:T(8,128)(2,1)S(1)}, u32[]{:S(2)}, u32[]{:S(2)}) async-start(bf16[8,64,128]{2,1,0:T(8,128)(2,1)} %bitcast.1), calls=%async_computation | async-start | bytes 262144 | tf_op jit(solution)/shard_map/cond/branch_1_fun/all_to_all | solution.py:127
  85.9 6.3 %collective-permute-start = (bf16[4,512,256]{2,1,0:T(8,128)(2,1)S(1)}, bf16[4,512,256]{2,1,0:T(8,128)(2,1)S(1)}, u32[]{:S(2)}, u32[]{:S(2)}) collective-permute-start(bf16[4,512,256]{2,1,0:T(8,128)(2,1)S(1)} %get-tuple-element.26.own_ref), channel_id=1, source_target_pairs={{0,16},{16,0},{1,17},{17,1},{2,18},{18,2},{3,19},{19,3},{4,20},{20... | collective-permute-start | bytes 3145736 | tf_op jit(solution)/shard_map/ppermute | solution.py:158
  92.2 1.9 %copy-start = (bf16[64,48,512]{2,1,0:T(8,128)(2,1)S(1)}, bf16[64,48,512]{2,1,0:T(8,128)(2,1)}, u32[]{:S(2)}) copy-start(bf16[64,48,512]{2,1,0:T(8,128)(2,1)} %all-gather.3.cloned.1.call-done) | copy-start | bytes 9437188
Sparse Core Ops, SparseCore 0:
  16.8 75.1 all-gather.2

commit v6 on v5

--- a/solution.py
+++ b/solution.py
@@ -146,15 +146,9 @@
     states = block_states(keys, values)
     index = lax.axis_index(CTX).astype(jnp.int32).reshape(1)
 
-    def gathered(states):
-        prefix = earlier_states(states)
-        attended = attend(index, queries, keys, values, prefix, groups)
-        return lax.all_to_all(attended, "x", 0, 0)
-
-    def nothing(states):
-        return jnp.zeros((groups, width, tokens), BF16)
-
-    attended = lax.cond(lax.axis_index(CTX) < 64, gathered, nothing, states)
+    prefix = earlier_states(states)
+    attended = attend(index, queries, keys, values, prefix, groups)
+    attended = lax.all_to_all(attended, "x", 0, 0)
     other = lax.ppermute(attended, "core", [(0, 1), (1, 0)])
     core = lax.axis_index("core").astype(jnp.int32).reshape(1)
     partial = project(core, weight, attended, other)

time: 133 us -> 133 us (level)
  blocking collectives: 87.5 us -> 72 us
  starting transfers between devices: 14.4 us -> 22.3 us
  waiting for transfers between devices: 8.12 us -> 14.6 us
  local copies, waits for them, and re-layouts: 1.89 us -> 4.75 us
  Pallas kernels: 6.45 us -> 4.32 us
    all_to_all x2 -> x1, blocking collectives: 30.2 us -> 15.8 us  [per_device(): attended = lax.all_to_all(attended, 'x', 0, 0)]
    all_to_all x0 -> x1, starting transfers between devices: none -> 7.39 us  [earlier_states(): return lax.all_to_all(prefix, NEAR, 0, 0).reshape(state.shape)]
    all_to_all x0 -> x1, waiting for transfers between devices: none -> 6.48 us  [earlier_states(): return lax.all_to_all(prefix, NEAR, 0, 0).reshape(state.shape)]
    unnamed x2 -> x12, local copies, waits for them, and re-layouts: 1.89 us -> 4.75 us
    all_to_all x1, blocking collectives: 28.4 us -> 27.1 us  [per_device(): lax.all_to_all(partial.reshape(32, columns, tokens), ('core',) + HEAD, 0, 0)]
  transfers between devices with their start and end apart: 3 -> 4, of which waited for: 2 -> 3; matrix products, arithmetic and copies ran while one was open for 0% -> 1% of each run, Pallas kernels for 3% -> 1%
where the time goes in v6:
time: 133 us; the launch traced here: 132 us
  blocking collectives  72 us (54%)
  starting transfers between devices  22.3 us (17%)
  waiting for transfers between devices  14.6 us (11%)
  between operations  13.4 us (10%)
  local copies, waits for them, and re-layouts  4.75 us (4%)
  Pallas kernels  4.32 us (3%)
    all_to_all x1, blocking collectives, per_device(): lax.all_to_all(partial.reshape(32, columns, tokens), ('core',) + HEAD, 0, 0)  27.1 us
    all_gather x1, blocking collectives, earlier_states(): totals = lax.all_gather(total, 'za')  18.8 us
    all_to_all x1, blocking collectives, per_device(): attended = lax.all_to_all(attended, 'x', 0, 0)  15.8 us
    all_to_all x1, starting transfers between devices, earlier_states(): pieces = lax.all_to_all(state.reshape(8, rows, DH), NEAR, 0, 0)  10.4 us
    all_to_all x1, blocking collectives, per_device(): lax.all_to_all(out_weight.T.reshape(groups, columns, width), 'x', 0, 0)  10.3 us
    all_to_all x1, starting transfers between devices, earlier_states(): return lax.all_to_all(prefix, NEAR, 0, 0).reshape(state.shape)  7.39 us
    all_to_all x1, waiting for transfers between devices, earlier_states(): return lax.all_to_all(prefix, NEAR, 0, 0).reshape(state.shape)  6.48 us
    all_to_all x1, waiting for transfers between devices, earlier_states(): pieces = lax.all_to_all(state.reshape(8, rows, DH), NEAR, 0, 0)  5.84 us
  transfers between devices with their start and end apart: 4, of which 3 were waited for; matrix products, arithmetic and copies ran while one was open for 1% of the time, Pallas kernels for 1%

profile of v6, /device:TPU:1, one launch (start us, length us, event | category | flops | bytes accessed | tf_op | source)
XLA Modules:
  0.0 132.3 jit_solution(6846438573720906807)
XLA Ops:
  6.5 0.0 copy-start.4
  6.5 0.0 copy-start.2
  6.5 0.0 all-gather.3.cloned.1.call-start
  6.5 10.3 %all_to_all.25 = bf16[4,48,512]{2,1,0:T(8,128)(2,1)} all-to-all(bf16[4,48,512]{2,1,0:T(8,128)(2,1)} %bitcast.14), channel_id=1, replica_groups=mesh['za'=4,'zb'=2,'zc'=2,'core'=2,'y'=4,'x'=4] {'x'}, dimensions={0} | all-to-all | bytes 393216 | tf_op jit(solution)/shard_map/all_to_all | solution.py:143
  16.8 0.0 all-gather.3.cloned.1.call-update
  16.8 0.0 copy-start.1
  16.8 0.9 copy-done.1
  17.8 0.0 copy-start.3
  17.8 0.9 copy-done.3
  18.7 0.9 block_state.1
  19.7 10.4 %all-to-all-start.1 = ((bf16[8,64,128]{2,1,0:T(8,128)(2,1)}), bf16[8,64,128]{2,1,0:T(8,128)(2,1)S(1)}, u32[]{:S(2)}, u32[]{:S(2)}) async-start(bf16[8,64,128]{2,1,0:T(8,128)(2,1)} %bitcast.5), calls=%async_computation.1 | async-start | bytes 262144 | tf_op jit(solution)/shard_map/all_to_all | solution.py:127
  30.1 5.8 %all-to-all-done.1 = bf16[8,64,128]{2,1,0:T(8,128)(2,1)S(1)} async-done(((bf16[8,64,128]{2,1,0:T(8,128)(2,1)}), bf16[8,64,128]{2,1,0:T(8,128)(2,1)S(1)}, u32[]{:S(2)}, u32[]{:S(2)}) %all-to-all-start.1) | async-done | bytes 131104 | tf_op jit(solution)/shard_map/all_to_all | solution.py:127
  35.9 18.8 %all_gather.11 = f32[4,64,128]{2,1,0:T(8,128)S(1)} all-gather(f32[1,64,128]{2,1,0:T(8,128)S(1)} %slice.4), channel_id=1, replica_groups=mesh['za'=4,'zb'=2,'zc'=2,'core'=2,'y'=4,'x'=4] {'za'}, dimensions={0}, use_global_device_ids=true | all-gather | bytes 163840 | tf_op jit(solution)/shard_map/all_gather | solution.py:132
  54.8 0.1 select_reduce_fusion
  54.8 0.7 fusion.3
  55.6 7.4 %all-to-all-start.2 = ((bf16[8,64,128]{2,1,0:T(8,128)(2,1)}), bf16[8,64,128]{2,1,0:T(8,128)(2,1)S(1)}, u32[]{:S(2)}, u32[]{:S(2)}) async-start(bf16[8,64,128]{2,1,0:T(8,128)(2,1)} %fusion.3), calls=%async_computation.2 | async-start | bytes 262144 | tf_op jit(solution)/shard_map/all_to_all | solution.py:136
  62.9 6.5 %all-to-all-done.2 = bf16[8,64,128]{2,1,0:T(8,128)(2,1)S(1)} async-done(((bf16[8,64,128]{2,1,0:T(8,128)(2,1)}), bf16[8,64,128]{2,1,0:T(8,128)(2,1)S(1)}, u32[]{:S(2)}, u32[]{:S(2)}) %all-to-all-start.2) | async-done | bytes 131104 | tf_op jit(solution)/shard_map/all_to_all | solution.py:136
  69.4 0.0 copy-done.4
  69.4 0.0 copy-done.2
  69.4 0.0 copy-start.5
  69.4 1.0 copy-done.5
  70.4 0.8 attend.1
  71.2 15.8 %all_to_all.26.own_ref = bf16[4,512,256]{2,1,0:T(8,128)(2,1)S(1)} all-to-all(bf16[4,512,256]{2,1,0:T(8,128)(2,1)S(1)} %attend.1), channel_id=1, replica_groups=mesh['za'=4,'zb'=2,'zc'=2,'core'=2,'y'=4,'x'=4] {'x'}, dimensions={0} | all-to-all | bytes 2097152 | tf_op jit(solution)/shard_map/all_to_all | solution.py:151
  87.0 4.5 %collective-permute-start = (bf16[4,512,256]{2,1,0:T(8,128)(2,1)S(1)}, bf16[4,512,256]{2,1,0:T(8,128)(2,1)S(1)}, u32[]{:S(2)}, u32[]{:S(2)}) collective-permute-start(bf16[4,512,256]{2,1,0:T(8,128)(2,1)S(1)} %all_to_all.26.own_ref), channel_id=1, source_target_pairs={{0,16},{16,0},{1,17},{17,1},{2,18},{18,2},{3,19},{19,3},{4,20},{20... | collective-permute-start | bytes 3145736 | tf_op jit(solution)/shard_map/ppermute | solution.py:152
  91.5 2.3 %collective-permute-done.other_ref = bf16[4,512,256]{2,1,0:T(8,128)(2,1)S(1)} collective-permute-done((bf16[4,512,256]{2,1,0:T(8,128)(2,1)S(1)}, bf16[4,512,256]{2,1,0:T(8,128)(2,1)S(1)}, u32[]{:S(2)}, u32[]{:S(2)}) %collective-permute-start) | collective-permute-done | bytes 1048608 | tf_op jit(solution)/shard_map/ppermute | solution.py:152
  93.8 0.0 all-gather.3.cloned.1.call-done
  93.8 0.0 copy-start
  93.8 1.9 %copy-done = bf16[64,48,512]{2,1,0:T(8,128)(2,1)S(1)} copy-done((bf16[64,48,512]{2,1,0:T(8,128)(2,1)S(1)}, bf16[64,48,512]{2,1,0:T(8,128)(2,1)}, u32[]{:S(2)}) %copy-start) | copy-done | bytes 3145752
  95.7 1.8 %project.1 = bf16[2,16,48,256]{3,2,1,0:T(8,128)(2,1)S(1)} custom-call(s32[1]{0:T(128)} %bitcast.core_ref, bf16[16,4,48,512]{3,2,1,0:T(8,128)(2,1)S(1)} %bitcast.11, bf16[4,512,256]{2,1,0:T(8,128)(2,1)S(1)} %all_to_all.26.own_ref, bf16[4,512,256]{2,1,0:T(8,128)(2,1)S(1)} %collective-permute-done.other_ref), custom_call_target="tpu_custom_call" | custom-call | tf_op jit(solution)/shard_map/project/pallas_call | solution.py:87
  97.5 27.1 %all_to_all.27 = bf16[32,48,256]{2,1,0:T(8,128)(2,1)S(1)} all-to-all(bf16[32,48,256]{2,1,0:T(8,128)(2,1)S(1)} %bitcast.10), channel_id=1, replica_groups=mesh['za'=4,'zb'=2,'zc'=2,'core'=2,'y'=4,'x'=4] {'core','y','x'}, dimensions={0} | all-to-all | bytes 1572864 | tf_op jit(solution)/shard_map/all_to_all | solution.py:155
  124.6 0.8 finish.1
  (3 shorter events, 0.0 us)
Async XLA Ops:
  6.5 62.9 %copy-start.4 = (bf16[256,512]{1,0:T(8,128)(2,1)S(1)}, bf16[256,512]{1,0:T(8,128)(2,1)}, u32[]{:S(2)}) copy-start(bf16[256,512]{1,0:T(8,128)(2,1)} %v_ref.3) | copy-start | bytes 786436
  6.5 62.9 %copy-start.2 = (bf16[256,512]{1,0:T(8,128)(2,1)S(1)}, bf16[256,512]{1,0:T(8,128)(2,1)}, u32[]{:S(2)}) copy-start(bf16[256,512]{1,0:T(8,128)(2,1)} %k_ref.3) | copy-start | bytes 786436
  6.5 87.3 %all-gather.3.cloned.1.call-start = ((), (), s32[]{:S(2)}) async-start(), calls=%async_computation.5 | async-start | bytes 3342336 | tf_op jit(solution)/shard_map/all_gather | solution.py:144
  16.8 1.0 copy-start.1
  17.8 0.9 copy-start.3
  19.7 16.3 %all-to-all-start.1 = ((bf16[8,64,128]{2,1,0:T(8,128)(2,1)}), bf16[8,64,128]{2,1,0:T(8,128)(2,1)S(1)}, u32[]{:S(2)}, u32[]{:S(2)}) async-start(bf16[8,64,128]{2,1,0:T(8,128)(2,1)} %bitcast.5), calls=%async_computation.1 | async-start | bytes 262144 | tf_op jit(solution)/shard_map/all_to_all | solution.py:127
  55.6 13.9 %all-to-all-start.2 = ((bf16[8,64,128]{2,1,0:T(8,128)(2,1)}), bf16[8,64,128]{2,1,0:T(8,128)(2,1)S(1)}, u32[]{:S(2)}, u32[]{:S(2)}) async-start(bf16[8,64,128]{2,1,0:T(8,128)(2,1)} %fusion.3), calls=%async_computation.2 | async-start | bytes 262144 | tf_op jit(solution)/shard_map/all_to_all | solution.py:136
  69.4 1.0 copy-start.5
  87.0 6.8 %collective-permute-start = (bf16[4,512,256]{2,1,0:T(8,128)(2,1)S(1)}, bf16[4,512,256]{2,1,0:T(8,128)(2,1)S(1)}, u32[]{:S(2)}, u32[]{:S(2)}) collective-permute-start(bf16[4,512,256]{2,1,0:T(8,128)(2,1)S(1)} %all_to_all.26.own_ref), channel_id=1, source_target_pairs={{0,16},{16,0},{1,17},{17,1},{2,18},{18,2},{3,19},{19,3},{4,20},{20... | collective-permute-start | bytes 3145736 | tf_op jit(solution)/shard_map/ppermute | solution.py:152
  93.8 1.9 %copy-start = (bf16[64,48,512]{2,1,0:T(8,128)(2,1)S(1)}, bf16[64,48,512]{2,1,0:T(8,128)(2,1)}, u32[]{:S(2)}) copy-start(bf16[64,48,512]{2,1,0:T(8,128)(2,1)} %all-gather.3.cloned.1.call-done) | copy-start | bytes 9437188
Sparse Core Ops, SparseCore 0:
  16.9 75.3 all-gather.2

commit v7 on v3

--- a/solution.py
+++ b/solution.py
@@ -11,11 +11,13 @@
 DH = 128
 BF16 = jnp.bfloat16
 F32 = jnp.float32
-GRID = {"za": 4, "zb": 2, "zc": 2, "core": 2, "y": 4, "x": 4}
+GRID = {"za": 4, "zb": 2, "zc": 2, "core": 2, "y": 4, "xh": 2, "xl": 2}
 AXES = tuple(GRID)
 CTX = ("za", "zb", "zc", "core")
-HEAD = ("y", "x")
+HEAD = ("y", "xh", "xl")
+PAIRS = ("zc", "xl")
 NEAR = ("zb", "zc", "core")
+FAR = "za"
 VMEM = pltpu.CompilerParams(vmem_limit_bytes=32 * 1024 * 1024)
 
 
@@ -68,36 +70,40 @@
 
 
 def project_kernel(w_ref, a_ref, out_ref):
-    shards, groups, columns, width = w_ref.shape
-    together = 8
-    rows = together * columns
-    for i in range(0, shards, together):
-        total = dot(w_ref[i : i + together, 0].reshape(rows, width), a_ref[0], ((1,), (0,)))
-        for g in range(1, groups):
-            part = w_ref[i : i + together, g].reshape(rows, width)
-            total += dot(part, a_ref[g], ((1,), (0,)))
-        out_ref[pl.ds(i * columns, rows), :] = total.astype(BF16)
+    pairs, halves, ends, groups, columns, width = w_ref.shape
+    for t in range(a_ref.shape[0]):
+        for half in range(halves):
+            for end in range(ends):
+                total = jnp.zeros((pairs * columns, a_ref.shape[3]), F32)
+                for g in range(groups):
+                    part = w_ref[:, half, end, g].reshape(pairs * columns, width)
+                    total += dot(part, a_ref[t, g], ((1,), (0,)))
+                out_ref[t, :, end, half] = total.astype(BF16).reshape(pairs, columns, -1)
 
 
 def project(weight, attended):
-    shards, groups, columns, width = weight.shape
+    pairs, halves, ends, _, columns, _ = weight.shape
+    blocks, _, _, tokens = attended.shape
     return pl.pallas_call(
         project_kernel,
-        out_shape=jax.ShapeDtypeStruct((shards * columns, attended.shape[2]), BF16),
+        out_shape=jax.ShapeDtypeStruct((blocks, pairs, ends, halves, columns, tokens), BF16),
         compiler_params=VMEM,
         name="project",
     )(weight, attended)
 
 
 def finish_kernel(parts_ref, out_ref):
-    for half in range(parts_ref.shape[2]):
-        for x in range(parts_ref.shape[1]):
-            total = parts_ref[0, x, half].astype(F32)
-            for y in range(1, parts_ref.shape[0]):
-                total += parts_ref[y, x, half].astype(F32)
-            columns = total.shape[0]
-            place = (half * parts_ref.shape[1] + x) * columns
-            out_ref[pl.ds(place, columns), :] = total
+    ends, ys, xhs, xls, halves, columns, _ = parts_ref.shape
+    for half in range(halves):
+        for end in range(ends):
+            for xl in range(xls):
+                total = None
+                for y in range(ys):
+                    for xh in range(xhs):
+                        part = parts_ref[end, y, xh, xl, half].astype(F32)
+                        total = part if total is None else total + part
+                place = ((half * ends + end) * xls + xl) * columns
+                out_ref[pl.ds(place, columns), :] = total
 
 
 def turn_kernel(parts_ref, out_ref, total_ref):
@@ -106,8 +112,8 @@
 
 
 def finish(parts):
-    _, x, halves, columns, tokens = parts.shape
-    total = x * halves * columns
+    ends, _, _, xls, halves, columns, tokens = parts.shape
+    total = ends * xls * halves * columns
     return pl.pallas_call(
         turn_kernel,
         out_shape=jax.ShapeDtypeStruct((tokens, total), BF16),
@@ -118,14 +124,13 @@
 
 
 def earlier_states(state):
-    rows = state.shape[0] // 8
-    pieces = lax.all_to_all(state.reshape(8, rows, DH), NEAR, 0, 0)
-    pieces = pieces.astype(F32)
+    near = lax.axis_size(NEAR)
+    pieces = lax.all_to_all(state.reshape(near, state.shape[0] // near, DH), NEAR, 0, 0).astype(F32)
     running = jnp.cumsum(pieces, axis=0)
     total = running[-1]
     before = running - pieces
-    totals = lax.all_gather(total.astype(BF16), "za").astype(F32)
-    reached = jnp.arange(GRID["za"])[:, None, None] < lax.axis_index("za")
+    totals = lax.all_gather(total.astype(BF16), FAR).astype(F32)
+    reached = jnp.arange(totals.shape[0])[:, None, None] < lax.axis_index(FAR)
     carried = jnp.sum(jnp.where(reached, totals, 0.0), axis=0)
     prefix = (before + carried[None]).astype(BF16)
     return lax.all_to_all(prefix, NEAR, 0, 0).reshape(state.shape)
@@ -133,27 +138,23 @@
 
 def per_device(queries, keys, values, out_weight):
     tokens, width = queries.shape
-    groups = GRID["x"]
+    groups = GRID["zc"] * GRID["xl"]
     columns = out_weight.shape[1] // groups
-    weight = lax.all_to_all(out_weight.T.reshape(groups, columns, width), "x", 0, 0)
-    weight = lax.all_gather(weight, CTX)
+    weight = lax.all_to_all(out_weight.T.reshape(groups, columns, width), PAIRS, 0, 0)
+    states = block_states(keys, values)
+    weight, states = lax.optimization_barrier((weight, states))
+    weight = lax.all_gather(weight, ("za", "zb", "core"))
+    weight = weight.reshape(8, 2, GRID["zc"], GRID["xl"], columns, width)
 
-    states = block_states(keys, values)
     index = lax.axis_index(CTX).astype(jnp.int32).reshape(1)
 
-    def gathered(states):
-        prefix = earlier_states(states)
-        attended = attend(index, queries, keys, values, prefix, groups)
-        return lax.all_to_all(attended, "x", 0, 0)
-
-    def nothing(states):
-        return jnp.zeros((groups, width, tokens), BF16)
-
-    attended = lax.cond(lax.axis_index(CTX) < 64, gathered, nothing, states)
+    prefix = earlier_states(states)
+    attended = attend(index, queries, keys, values, prefix, groups)
+    attended = lax.all_to_all(attended, PAIRS, 0, 0)
+    attended = attended.reshape(GRID["zc"], GRID["xl"], width, tokens)
     partial = project(weight, attended)
-    owners = GRID["y"] * GRID["x"]
-    parts = lax.all_to_all(partial.reshape(owners, 2 * columns, tokens), HEAD, 0, 0)
-    return finish(parts.reshape(GRID["y"], GRID["x"], 2, columns, tokens))
+    parts = lax.all_to_all(partial.reshape(32, 2 * columns, tokens), ("zc",) + HEAD, 0, 0)
+    return finish(parts.reshape(2, GRID["y"], GRID["xh"], GRID["xl"], 2, columns, tokens))
 
 
 def solution(mesh):

time: 134 us -> 131 us (0.978)
  starting transfers between devices: 10.4 us -> 22.1 us
  waiting for transfers between devices: 22.8 us -> 14.8 us
  blocking collectives: 77.3 us -> 69.9 us
  Pallas kernels: 6.45 us -> 4.42 us
  local copies, waits for them, and re-layouts: 2.79 us -> 4.48 us
    all_gather x1, waiting for transfers between devices: 16.9 us -> 0.01 us  [per_device(): weight = lax.all_gather(weight, ('za', 'zb', 'core'))]
    all_to_all x1 -> x3, starting transfers between devices: 10.4 us -> 22.1 us  [the longest x1 9.99 us: earlier_states(): lax.all_to_all(state.reshape(near, state.shape[0] // near, DH), NEAR, 0, 0)]
    all_to_all x1 -> x3, waiting for transfers between devices: 5.84 us -> 14.8 us  [the longest x1 7.75 us: earlier_states(): return lax.all_to_all(prefix, NEAR, 0, 0).reshape(state.shape)]
    all_to_all x4 -> x2, blocking collectives: 59.2 us -> 52.1 us  [the longest x1 28.5 us: per_device(): lax.all_to_all(partial.reshape(32, 2 * columns, tokens), ('zc',) + HEAD,...]
    unnamed x2 -> x14, local copies, waits for them, and re-layouts: 2.78 us -> 4.48 us
  transfers between devices with their start and end apart: 2 -> 4, of which waited for: 2 -> 3; matrix products, arithmetic and copies ran while one was open for 0% -> 1% of each run, Pallas kernels for 3% -> 1%
where the time goes in v7:
time: 131 us; the launch traced here: 130 us
  blocking collectives  69.9 us (53%)
  starting transfers between devices  22.1 us (17%)
  waiting for transfers between devices  14.8 us (11%)
  between operations  13.4 us (10%)
  local copies, waits for them, and re-layouts  4.48 us (3%)
  Pallas kernels  4.42 us (3%)
    all_to_all x1, blocking collectives, per_device(): lax.all_to_all(partial.reshape(32, 2 * columns, tokens), ('zc',) + HEAD,...  28.5 us
    all_to_all x1, blocking collectives, per_device(): attended = lax.all_to_all(attended, PAIRS, 0, 0)  23.6 us
    all_gather x1, blocking collectives, earlier_states(): totals = lax.all_gather(total.astype(BF16), FAR).astype(F32)  17.8 us
    all_to_all x1, starting transfers between devices, earlier_states(): lax.all_to_all(state.reshape(near, state.shape[0] // near, DH), NEAR, 0, 0)  9.99 us
    all_to_all x1, waiting for transfers between devices, earlier_states(): return lax.all_to_all(prefix, NEAR, 0, 0).reshape(state.shape)  7.75 us
    all_to_all x1, starting transfers between devices, earlier_states(): return lax.all_to_all(prefix, NEAR, 0, 0).reshape(state.shape)  7.36 us
    all_to_all x1, waiting for transfers between devices, earlier_states(): lax.all_to_all(state.reshape(near, state.shape[0] // near, DH), NEAR, 0, 0)  5.84 us
    all_to_all x1, starting transfers between devices, per_device(): lax.all_to_all(out_weight.T.reshape(groups, columns, width), PAIRS, 0, 0)  4.79 us
  transfers between devices with their start and end apart: 4, of which 3 were waited for; matrix products, arithmetic and copies ran while one was open for 1% of the time, Pallas kernels for 1%

profile of v7, /device:TPU:1, one launch (start us, length us, event | category | flops | bytes accessed | tf_op | source)
XLA Modules:
  0.0 130.0 jit_solution(8081465555874813010)
XLA Ops:
  6.5 0.0 copy-start.2
  6.5 4.8 %all-to-all-start = ((bf16[4,48,512]{2,1,0:T(8,128)(2,1)}), bf16[4,48,512]{2,1,0:T(8,128)(2,1)S(1)}, u32[]{:S(2)}, u32[]{:S(2)}) async-start(bf16[4,48,512]{2,1,0:T(8,128)(2,1)} %bitcast.15), calls=%async_computation | async-start | bytes 393216 | tf_op jit(solution)/shard_map/all_to_all | solution.py:143
  11.3 0.0 all-gather.3.cloned.1.call-start
  11.3 0.0 copy-start.1
  11.3 0.9 copy-done.1
  12.3 0.0 copy-start.3
  12.3 0.9 copy-done.3
  13.2 0.0 copy-start.4
  13.2 0.0 copy-start.5
  13.2 0.9 block_state.1
  14.2 1.2 all-to-all-done
  15.4 0.0 copy-start.6
  15.4 0.7 copy-done.6
  16.1 0.0 all-gather.3.cloned.1.call-update
  16.1 10.0 %all-to-all-start.1 = ((bf16[8,64,128]{2,1,0:T(8,128)(2,1)}), bf16[8,64,128]{2,1,0:T(8,128)(2,1)S(1)}, u32[]{:S(2)}, u32[]{:S(2)}) async-start(bf16[8,64,128]{2,1,0:T(8,128)(2,1)} %bitcast.4), calls=%async_computation.1 | async-start | bytes 262144 | tf_op jit(solution)/shard_map/all_to_all | solution.py:128
  26.1 5.8 %all-to-all-done.1 = bf16[8,64,128]{2,1,0:T(8,128)(2,1)S(1)} async-done(((bf16[8,64,128]{2,1,0:T(8,128)(2,1)}), bf16[8,64,128]{2,1,0:T(8,128)(2,1)S(1)}, u32[]{:S(2)}, u32[]{:S(2)}) %all-to-all-start.1) | async-done | bytes 131104 | tf_op jit(solution)/shard_map/all_to_all | solution.py:128
  31.9 17.8 %all_gather.12 = bf16[4,64,128]{2,1,0:T(8,128)(2,1)S(1)} all-gather(bf16[1,64,128]{2,1,0:T(8,128)(2,1)S(1)} %slice.7), channel_id=1, replica_groups=mesh['za'=4,'zb'=2,'zc'=2,'core'=2,'y'=4,'xh'=2,'xl'=2] {'za'}, dimensions={0}, use_global_device_ids=true | all-gather | bytes 81920 | tf_op jit(solution)/shard_map/all_gather | solution.py:132
  49.7 0.1 select_reduce_fusion
  49.8 0.7 fusion.3
  50.5 7.4 %all-to-all-start.2 = ((bf16[8,64,128]{2,1,0:T(8,128)(2,1)}), bf16[8,64,128]{2,1,0:T(8,128)(2,1)S(1)}, u32[]{:S(2)}, u32[]{:S(2)}) async-start(bf16[8,64,128]{2,1,0:T(8,128)(2,1)} %fusion.3), calls=%async_computation.2 | async-start | bytes 262144 | tf_op jit(solution)/shard_map/all_to_all | solution.py:136
  57.9 7.7 %all-to-all-done.2 = bf16[8,64,128]{2,1,0:T(8,128)(2,1)S(1)} async-done(((bf16[8,64,128]{2,1,0:T(8,128)(2,1)}), bf16[8,64,128]{2,1,0:T(8,128)(2,1)S(1)}, u32[]{:S(2)}, u32[]{:S(2)}) %all-to-all-start.2) | async-done | bytes 131104 | tf_op jit(solution)/shard_map/all_to_all | solution.py:136
  65.6 0.0 copy-done.2
  65.6 0.0 copy-done.4
  65.6 0.0 copy-done.5
  65.6 0.8 attend.1
  66.4 23.6 %all_to_all.25 = bf16[4,512,256]{2,1,0:T(8,128)(2,1)S(1)} all-to-all(bf16[4,512,256]{2,1,0:T(8,128)(2,1)S(1)} %attend.1), channel_id=1, replica_groups=mesh['za'=4,'zb'=2,'zc'=2,'core'=2,'y'=4,'xh'=2,'xl'=2] {'zc','xl'}, dimensions={0} | all-to-all | bytes 2097152 | tf_op jit(solution)/shard_map/all_to_all | solution.py:153
  90.1 0.0 all-gather.3.cloned.1.call-done
  90.1 0.0 copy-start
  90.1 1.9 %copy-done = bf16[64,48,512]{2,1,0:T(8,128)(2,1)S(1)} copy-done((bf16[64,48,512]{2,1,0:T(8,128)(2,1)S(1)}, bf16[64,48,512]{2,1,0:T(8,128)(2,1)}, u32[]{:S(2)}) %copy-start) | copy-done | bytes 3145752
  91.9 1.8 %project.1 = bf16[2,8,2,2,48,256]{5,4,3,2,1,0:T(8,128)(2,1)S(1)} custom-call(bf16[8,2,2,2,48,512]{5,4,3,2,1,0:T(8,128)(2,1)S(1)} %bitcast.13, bf16[2,2,512,256]{3,2,1,0:T(8,128)(2,1)S(1)} %bitcast.12), custom_call_target="tpu_custom_call" | custom-call | tf_op jit(solution)/shard_map/project/pallas_call | solution.py:87
  93.7 28.5 %all_to_all.26 = bf16[32,96,256]{2,1,0:T(8,128)(2,1)S(1)} all-to-all(bf16[32,96,256]{2,1,0:T(8,128)(2,1)S(1)} %bitcast.11), channel_id=1, replica_groups=mesh['za'=4,'zb'=2,'zc'=2,'core'=2,'y'=4,'xh'=2,'xl'=2] {'zc','y','xh','..., dimensions={0} | all-to-all | bytes 3145728 | tf_op jit(solution)/shard_map/all_to_all | solution.py:156
  122.2 0.9 finish.1
  (3 shorter events, 0.0 us)
Async XLA Ops:
  6.5 59.1 %copy-start.2 = (bf16[256,512]{1,0:T(8,128)(2,1)S(1)}, bf16[256,512]{1,0:T(8,128)(2,1)}, u32[]{:S(2)}) copy-start(bf16[256,512]{1,0:T(8,128)(2,1)} %k_ref.3) | copy-start | bytes 786436
  6.5 8.8 %all-to-all-start = ((bf16[4,48,512]{2,1,0:T(8,128)(2,1)}), bf16[4,48,512]{2,1,0:T(8,128)(2,1)S(1)}, u32[]{:S(2)}, u32[]{:S(2)}) async-start(bf16[4,48,512]{2,1,0:T(8,128)(2,1)} %bitcast.15), calls=%async_computation | async-start | bytes 393216 | tf_op jit(solution)/shard_map/all_to_all | solution.py:143
  11.3 78.7 %all-gather.3.cloned.1.call-start = ((), (), s32[]{:S(2)}) async-start(), calls=%async_computation.5 | async-start | bytes 3342336 | tf_op jit(solution)/shard_map/all_gather | solution.py:146
  11.3 0.9 copy-start.1
  12.3 0.9 copy-start.3
  13.2 52.4 %copy-start.4 = (bf16[256,512]{1,0:T(8,128)(2,1)S(1)}, bf16[256,512]{1,0:T(8,128)(2,1)}, u32[]{:S(2)}) copy-start(bf16[256,512]{1,0:T(8,128)(2,1)} %v_ref.3) | copy-start | bytes 786436
  13.2 52.4 %copy-start.5 = (bf16[256,512]{1,0:T(8,128)(2,1)S(1)}, bf16[256,512]{1,0:T(8,128)(2,1)}, u32[]{:S(2)}) copy-start(bf16[256,512]{1,0:T(8,128)(2,1)} %q_ref.1) | copy-start | bytes 786436
  15.4 0.7 copy-start.6
  16.1 15.8 %all-to-all-start.1 = ((bf16[8,64,128]{2,1,0:T(8,128)(2,1)}), bf16[8,64,128]{2,1,0:T(8,128)(2,1)S(1)}, u32[]{:S(2)}, u32[]{:S(2)}) async-start(bf16[8,64,128]{2,1,0:T(8,128)(2,1)} %bitcast.4), calls=%async_computation.1 | async-start | bytes 262144 | tf_op jit(solution)/shard_map/all_to_all | solution.py:128
  50.5 15.1 %all-to-all-start.2 = ((bf16[8,64,128]{2,1,0:T(8,128)(2,1)}), bf16[8,64,128]{2,1,0:T(8,128)(2,1)S(1)}, u32[]{:S(2)}, u32[]{:S(2)}) async-start(bf16[8,64,128]{2,1,0:T(8,128)(2,1)} %fusion.3), calls=%async_computation.2 | async-start | bytes 262144 | tf_op jit(solution)/shard_map/all_to_all | solution.py:136
  90.1 1.9 %copy-start = (bf16[64,48,512]{2,1,0:T(8,128)(2,1)S(1)}, bf16[64,48,512]{2,1,0:T(8,128)(2,1)}, u32[]{:S(2)}) copy-start(bf16[64,48,512]{2,1,0:T(8,128)(2,1)} %all-gather.3.cloned.1.call-done) | copy-start | bytes 9437188
Sparse Core Ops, SparseCore 0:
  16.2 68.6 all-gather.2

commit v8 on v7

--- a/solution.py
+++ b/solution.py
@@ -1,5 +1,3 @@
-import functools
-
 import jax
 import jax.numpy as jnp
 from jax import lax
@@ -16,7 +14,7 @@
 CTX = ("za", "zb", "zc", "core")
 HEAD = ("y", "xh", "xl")
 PAIRS = ("zc", "xl")
-NEAR = ("zb", "zc", "core")
+NEAR = ("zb", "zc")
 FAR = "za"
 VMEM = pltpu.CompilerParams(vmem_limit_bytes=32 * 1024 * 1024)
 
@@ -124,8 +122,13 @@
 
 
 def earlier_states(state):
+    core = lax.axis_index("core")
+    half = state.shape[0] // 2
+    both = lax.all_gather(state, "core")
+    mine = lax.dynamic_slice_in_dim(both, core * half, half, axis=1).astype(F32)
+    chip = jnp.sum(mine, axis=0).astype(BF16)
     near = lax.axis_size(NEAR)
-    pieces = lax.all_to_all(state.reshape(near, state.shape[0] // near, DH), NEAR, 0, 0).astype(F32)
+    pieces = lax.all_to_all(chip.reshape(near, half // near, DH), NEAR, 0, 0).astype(F32)
     running = jnp.cumsum(pieces, axis=0)
     total = running[-1]
     before = running - pieces
@@ -133,7 +136,9 @@
     reached = jnp.arange(totals.shape[0])[:, None, None] < lax.axis_index(FAR)
     carried = jnp.sum(jnp.where(reached, totals, 0.0), axis=0)
     prefix = (before + carried[None]).astype(BF16)
-    return lax.all_to_all(prefix, NEAR, 0, 0).reshape(state.shape)
+    prefix = lax.all_to_all(prefix, NEAR, 0, 0).reshape(half, DH)
+    prefix = lax.all_gather(prefix, "core", tiled=True).astype(F32)
+    return (prefix + jnp.where(core == 1, both[0].astype(F32), 0.0)).astype(BF16)
 
 
 def per_device(queries, keys, values, out_weight):

time: 131 us -> 131 us (level)
  blocking collectives: 69.9 us -> 84.2 us
  starting transfers between devices: 22.1 us -> 11.2 us
  waiting for transfers between devices: 14.8 us -> 11.5 us
    all_gather x0 -> x2, blocking collectives: none -> 14.4 us  [the longest x1 8.34 us: earlier_states(): both = lax.all_gather(state, 'core')]
    all_to_all x2, starting transfers between devices: 17.4 us -> 6.57 us  [the longest x1 3.28 us: earlier_states(): prefix = lax.all_to_all(prefix, NEAR, 0, 0).reshape(half, DH)]
    all_to_all x2, waiting for transfers between devices: 13.6 us -> 9.57 us  [the longest x1 4.93 us: earlier_states(): prefix = lax.all_to_all(prefix, NEAR, 0, 0).reshape(half, DH)]
    all_gather x1, blocking collectives: 17.8 us -> 19.9 us  [earlier_states(): totals = lax.all_gather(total.astype(BF16), FAR).astype(F32)]
where the time goes in v8:
time: 131 us; the launch traced here: 130 us
  blocking collectives  84.2 us (64%)
  between operations  13.5 us (10%)
  waiting for transfers between devices  11.5 us (9%)
  starting transfers between devices  11.2 us (9%)
  local copies, waits for them, and re-layouts  4.48 us (3%)
  Pallas kernels  3.76 us (3%)
  other arithmetic  1.42 us (1%)
    all_to_all x1, blocking collectives, per_device(): lax.all_to_all(partial.reshape(32, 2 * columns, tokens), ('zc',) + HEAD,...  27.6 us
    all_to_all x1, blocking collectives, per_device(): attended = lax.all_to_all(attended, PAIRS, 0, 0)  22.3 us
    all_gather x1, blocking collectives, earlier_states(): totals = lax.all_gather(total.astype(BF16), FAR).astype(F32)  19.9 us
    all_gather x1, blocking collectives, earlier_states(): both = lax.all_gather(state, 'core')  8.34 us
    all_gather x1, blocking collectives, earlier_states(): prefix = lax.all_gather(prefix, 'core', tiled=True).astype(F32)  6.02 us
    all_to_all x1, waiting for transfers between devices, earlier_states(): prefix = lax.all_to_all(prefix, NEAR, 0, 0).reshape(half, DH)  4.93 us
    all_to_all x1, starting transfers between devices, per_device(): lax.all_to_all(out_weight.T.reshape(groups, columns, width), PAIRS, 0, 0)  4.66 us
    all_to_all x1, waiting for transfers between devices, earlier_states(): lax.all_to_all(chip.reshape(near, half // near, DH), NEAR, 0, 0).astype(F32)  4.65 us
  transfers between devices with their start and end apart: 4, of which 3 were waited for; matrix products, arithmetic and copies ran while one was open for 1% of the time, Pallas kernels for 1%

profile of v8, /device:TPU:1, one launch (start us, length us, event | category | flops | bytes accessed | tf_op | source)
XLA Modules:
  0.0 130.0 jit_solution(16797106284851071770)
XLA Ops:
  6.5 4.7 %all-to-all-start = ((bf16[4,48,512]{2,1,0:T(8,128)(2,1)}), bf16[4,48,512]{2,1,0:T(8,128)(2,1)S(1)}, u32[]{:S(2)}, u32[]{:S(2)}) async-start(bf16[4,48,512]{2,1,0:T(8,128)(2,1)} %bitcast.17), calls=%async_computation | async-start | bytes 393216 | tf_op jit(solution)/shard_map/all_to_all | solution.py:148
  11.2 0.0 all-gather.4.cloned.1.call-start
  11.2 0.0 copy-start.1
  11.2 0.9 copy-done.1
  12.2 0.0 copy-start.3
  12.2 0.9 copy-done.3
  13.1 0.0 copy-start.2
  13.1 0.0 copy-start.4
  13.1 0.0 copy-start.5
  13.1 0.3 block_state.1
  13.4 1.9 %all-to-all-done = bf16[4,48,512]{2,1,0:T(8,128)(2,1)S(1)} async-done(((bf16[4,48,512]{2,1,0:T(8,128)(2,1)}), bf16[4,48,512]{2,1,0:T(8,128)(2,1)S(1)}, u32[]{:S(2)}, u32[]{:S(2)}) %all-to-all-start) | async-done | bytes 196640 | tf_op jit(solution)/shard_map/all_to_all | solution.py:148
  15.2 0.0 copy-start.6
  15.2 0.7 copy-done.6
  15.9 0.0 all-gather.4.cloned.1.call-update
  16.0 8.3 %all-gather.1 = bf16[1024,128]{1,0:T(8,128)(2,1)S(1)} all-gather(bf16[512,128]{1,0:T(8,128)(2,1)S(1)} %block_state.1), channel_id=3, replica_groups=mesh['za'=4,'zb'=2,'zc'=2,'core'=2,'y'=4,'xh'=2,'xl'=2] {'core'}, dimensions={0}, use_global_device_ids=true | all-gather | bytes 393216 | tf_op jit(solution)/shard_map/all_gather | solution.py:127
  24.3 0.6 dynamic-slice_reduce_fusion
  24.9 3.3 %all-to-all-start.1 = ((bf16[4,64,128]{2,1,0:T(8,128)(2,1)}), bf16[4,64,128]{2,1,0:T(8,128)(2,1)S(1)}, u32[]{:S(2)}, u32[]{:S(2)}) async-start(bf16[4,64,128]{2,1,0:T(8,128)(2,1)} %bitcast.5), calls=%async_computation.1 | async-start | bytes 131072 | tf_op jit(solution)/shard_map/all_to_all | solution.py:131
  28.2 4.6 %all-to-all-done.1 = bf16[4,64,128]{2,1,0:T(8,128)(2,1)S(1)} async-done(((bf16[4,64,128]{2,1,0:T(8,128)(2,1)}), bf16[4,64,128]{2,1,0:T(8,128)(2,1)S(1)}, u32[]{:S(2)}, u32[]{:S(2)}) %all-to-all-start.1) | async-done | bytes 65568 | tf_op jit(solution)/shard_map/all_to_all | solution.py:131
  32.9 19.9 %all_gather.23 = bf16[4,64,128]{2,1,0:T(8,128)(2,1)S(1)} all-gather(bf16[1,64,128]{2,1,0:T(8,128)(2,1)S(1)} %slice.14), channel_id=1, replica_groups=mesh['za'=4,'zb'=2,'zc'=2,'core'=2,'y'=4,'xh'=2,'xl'=2] {'za'}, dimensions={0}, use_global_device_ids=true | all-gather | bytes 81920 | tf_op jit(solution)/shard_map/all_gather | solution.py:135
  52.8 0.1 select_reduce_fusion
  52.9 0.6 fusion.4
  53.5 3.3 %all-to-all-start.2 = ((bf16[4,64,128]{2,1,0:T(8,128)(2,1)}), bf16[4,64,128]{2,1,0:T(8,128)(2,1)S(1)}, u32[]{:S(2)}, u32[]{:S(2)}) async-start(bf16[4,64,128]{2,1,0:T(8,128)(2,1)} %fusion.4), calls=%async_computation.2 | async-start | bytes 131072 | tf_op jit(solution)/shard_map/all_to_all | solution.py:139
  56.8 4.9 %all-to-all-done.2 = bf16[4,64,128]{2,1,0:T(8,128)(2,1)S(1)} async-done(((bf16[4,64,128]{2,1,0:T(8,128)(2,1)}), bf16[4,64,128]{2,1,0:T(8,128)(2,1)S(1)}, u32[]{:S(2)}, u32[]{:S(2)}) %all-to-all-start.2) | async-done | bytes 65568 | tf_op jit(solution)/shard_map/all_to_all | solution.py:139
  61.7 6.0 %all_gather.24 = bf16[512,128]{1,0:T(8,128)(2,1)S(1)} all-gather(bf16[256,128]{1,0:T(8,128)(2,1)S(1)} %bitcast.16), channel_id=1, replica_groups=mesh['za'=4,'zb'=2,'zc'=2,'core'=2,'y'=4,'xh'=2,'xl'=2] {'core'}, dimensions={0}, use_global_device_ids=true | all-gather | bytes 196608 | tf_op jit(solution)/shard_map/all_gather | solution.py:140
  67.8 0.0 copy-done.2
  67.8 0.0 copy-done.4
  67.8 0.0 copy-done.5
  67.8 0.8 attend.1
  68.6 22.3 %all_to_all.25 = bf16[4,512,256]{2,1,0:T(8,128)(2,1)S(1)} all-to-all(bf16[4,512,256]{2,1,0:T(8,128)(2,1)S(1)} %attend.1), channel_id=1, replica_groups=mesh['za'=4,'zb'=2,'zc'=2,'core'=2,'y'=4,'xh'=2,'xl'=2] {'zc','xl'}, dimensions={0} | all-to-all | bytes 2097152 | tf_op jit(solution)/shard_map/all_to_all | solution.py:158
  90.9 0.0 all-gather.4.cloned.1.call-done
  90.9 0.0 copy-start
  90.9 1.9 %copy-done = bf16[64,48,512]{2,1,0:T(8,128)(2,1)S(1)} copy-done((bf16[64,48,512]{2,1,0:T(8,128)(2,1)S(1)}, bf16[64,48,512]{2,1,0:T(8,128)(2,1)}, u32[]{:S(2)}) %copy-start) | copy-done | bytes 3145752
  92.8 1.8 %project.1 = bf16[2,8,2,2,48,256]{5,4,3,2,1,0:T(8,128)(2,1)S(1)} custom-call(bf16[8,2,2,2,48,512]{5,4,3,2,1,0:T(8,128)(2,1)S(1)} %bitcast.14, bf16[2,2,512,256]{3,2,1,0:T(8,128)(2,1)S(1)} %bitcast.13), custom_call_target="tpu_custom_call" | custom-call | tf_op jit(solution)/shard_map/project/pallas_call | solution.py:85
  94.6 27.6 %all_to_all.26 = bf16[32,96,256]{2,1,0:T(8,128)(2,1)S(1)} all-to-all(bf16[32,96,256]{2,1,0:T(8,128)(2,1)S(1)} %bitcast.12), channel_id=1, replica_groups=mesh['za'=4,'zb'=2,'zc'=2,'core'=2,'y'=4,'xh'=2,'xl'=2] {'zc','y','xh','..., dimensions={0} | all-to-all | bytes 3145728 | tf_op jit(solution)/shard_map/all_to_all | solution.py:161
  122.2 0.9 finish.1
  (4 shorter events, 0.1 us)
Async XLA Ops:
  6.5 8.7 %all-to-all-start = ((bf16[4,48,512]{2,1,0:T(8,128)(2,1)}), bf16[4,48,512]{2,1,0:T(8,128)(2,1)S(1)}, u32[]{:S(2)}, u32[]{:S(2)}) async-start(bf16[4,48,512]{2,1,0:T(8,128)(2,1)} %bitcast.17), calls=%async_computation | async-start | bytes 393216 | tf_op jit(solution)/shard_map/all_to_all | solution.py:148
  11.2 79.7 %all-gather.4.cloned.1.call-start = ((), (), s32[]{:S(2)}) async-start(), calls=%async_computation.5 | async-start | bytes 3342336 | tf_op jit(solution)/shard_map/all_gather | solution.py:151
  11.2 0.9 copy-start.1
  12.2 0.9 copy-start.3
  13.1 54.7 %copy-start.2 = (bf16[256,512]{1,0:T(8,128)(2,1)S(1)}, bf16[256,512]{1,0:T(8,128)(2,1)}, u32[]{:S(2)}) copy-start(bf16[256,512]{1,0:T(8,128)(2,1)} %k_ref.3) | copy-start | bytes 786436
  13.1 54.7 %copy-start.4 = (bf16[256,512]{1,0:T(8,128)(2,1)S(1)}, bf16[256,512]{1,0:T(8,128)(2,1)}, u32[]{:S(2)}) copy-start(bf16[256,512]{1,0:T(8,128)(2,1)} %v_ref.3) | copy-start | bytes 786436
  13.1 54.7 %copy-start.5 = (bf16[256,512]{1,0:T(8,128)(2,1)S(1)}, bf16[256,512]{1,0:T(8,128)(2,1)}, u32[]{:S(2)}) copy-start(bf16[256,512]{1,0:T(8,128)(2,1)} %q_ref.1) | copy-start | bytes 786436
  15.2 0.7 copy-start.6
  24.9 8.0 %all-to-all-start.1 = ((bf16[4,64,128]{2,1,0:T(8,128)(2,1)}), bf16[4,64,128]{2,1,0:T(8,128)(2,1)S(1)}, u32[]{:S(2)}, u32[]{:S(2)}) async-start(bf16[4,64,128]{2,1,0:T(8,128)(2,1)} %bitcast.5), calls=%async_computation.1 | async-start | bytes 131072 | tf_op jit(solution)/shard_map/all_to_all | solution.py:131
  53.5 8.2 %all-to-all-start.2 = ((bf16[4,64,128]{2,1,0:T(8,128)(2,1)}), bf16[4,64,128]{2,1,0:T(8,128)(2,1)S(1)}, u32[]{:S(2)}, u32[]{:S(2)}) async-start(bf16[4,64,128]{2,1,0:T(8,128)(2,1)} %fusion.4), calls=%async_computation.2 | async-start | bytes 131072 | tf_op jit(solution)/shard_map/all_to_all | solution.py:139
  90.9 1.9 %copy-start = (bf16[64,48,512]{2,1,0:T(8,128)(2,1)S(1)}, bf16[64,48,512]{2,1,0:T(8,128)(2,1)}, u32[]{:S(2)}) copy-start(bf16[64,48,512]{2,1,0:T(8,128)(2,1)} %all-gather.4.cloned.1.call-done) | copy-start | bytes 9437188
Sparse Core Ops, SparseCore 0:
  16.1 67.8 all-gather.3

commit v9 on v7

--- a/solution.py
+++ b/solution.py
@@ -1,5 +1,3 @@
-import functools
-
 import jax
 import jax.numpy as jnp
 from jax import lax
@@ -70,23 +68,27 @@
 
 
 def project_kernel(w_ref, a_ref, out_ref):
-    pairs, halves, ends, groups, columns, width = w_ref.shape
-    for t in range(a_ref.shape[0]):
+    blocks, groups, width, tokens = a_ref.shape
+    _, pairs, ends, halves, columns, _ = out_ref.shape
+    for t in range(blocks):
         for half in range(halves):
             for end in range(ends):
-                total = jnp.zeros((pairs * columns, a_ref.shape[3]), F32)
+                total = jnp.zeros((pairs * columns, tokens), F32)
                 for g in range(groups):
-                    part = w_ref[:, half, end, g].reshape(pairs * columns, width)
-                    total += dot(part, a_ref[t, g], ((1,), (0,)))
+                    row = (end * groups + g) * columns
+                    lanes = [(pair * halves + half) * width for pair in range(pairs)]
+                    parts = [w_ref[row : row + columns, lane : lane + width] for lane in lanes]
+                    total += dot(jnp.concatenate(parts, axis=0), a_ref[t, g], ((1,), (0,)))
                 out_ref[t, :, end, half] = total.astype(BF16).reshape(pairs, columns, -1)
 
 
 def project(weight, attended):
-    pairs, halves, ends, _, columns, _ = weight.shape
-    blocks, _, _, tokens = attended.shape
+    blocks, groups, width, tokens = attended.shape
+    columns = weight.shape[0] // (2 * groups)
+    pairs = weight.shape[1] // (2 * width)
     return pl.pallas_call(
         project_kernel,
-        out_shape=jax.ShapeDtypeStruct((blocks, pairs, ends, halves, columns, tokens), BF16),
+        out_shape=jax.ShapeDtypeStruct((blocks, pairs, 2, 2, columns, tokens), BF16),
         compiler_params=VMEM,
         name="project",
     )(weight, attended)
@@ -143,8 +145,8 @@
     weight = lax.all_to_all(out_weight.T.reshape(groups, columns, width), PAIRS, 0, 0)
     states = block_states(keys, values)
     weight, states = lax.optimization_barrier((weight, states))
-    weight = lax.all_gather(weight, ("za", "zb", "core"))
-    weight = weight.reshape(8, 2, GRID["zc"], GRID["xl"], columns, width)
+    weight = weight.reshape(groups * columns, width)
+    weight = lax.all_gather(weight, ("za", "zb", "core"), axis=1, tiled=True)
 
     index = lax.axis_index(CTX).astype(jnp.int32).reshape(1)
 

time: 131 us -> 131 us (level)
  no operation moved by 1% of the time
where the time goes in v9:
time: 131 us; the launch traced here: 130 us
  blocking collectives  69.4 us (53%)
  starting transfers between devices  22.1 us (17%)
  waiting for transfers between devices  15.2 us (12%)
  between operations  13.4 us (10%)
  local copies, waits for them, and re-layouts  4.48 us (3%)
  Pallas kernels  4.42 us (3%)
    all_to_all x1, blocking collectives, per_device(): lax.all_to_all(partial.reshape(32, 2 * columns, tokens), ('zc',) + HEAD,...  28.3 us
    all_to_all x1, blocking collectives, per_device(): attended = lax.all_to_all(attended, PAIRS, 0, 0)  23.3 us
    all_gather x1, blocking collectives, earlier_states(): totals = lax.all_gather(total.astype(BF16), FAR).astype(F32)  17.8 us
    all_to_all x1, starting transfers between devices, earlier_states(): lax.all_to_all(state.reshape(near, state.shape[0] // near, DH), NEAR, 0, 0)  9.99 us
    all_to_all x1, waiting for transfers between devices, earlier_states(): return lax.all_to_all(prefix, NEAR, 0, 0).reshape(state.shape)  8.16 us
    all_to_all x1, starting transfers between devices, earlier_states(): return lax.all_to_all(prefix, NEAR, 0, 0).reshape(state.shape)  7.37 us
    all_to_all x1, waiting for transfers between devices, earlier_states(): lax.all_to_all(state.reshape(near, state.shape[0] // near, DH), NEAR, 0, 0)  5.84 us
    all_to_all x1, starting transfers between devices, per_device(): lax.all_to_all(out_weight.T.reshape(groups, columns, width), PAIRS, 0, 0)  4.79 us
  transfers between devices with their start and end apart: 4, of which 3 were waited for; matrix products, arithmetic and copies ran while one was open for 1% of the time, Pallas kernels for 1%

profile of v9, /device:TPU:1, one launch (start us, length us, event | category | flops | bytes accessed | tf_op | source)
XLA Modules:
  0.0 129.9 jit_solution(12158325805623728285)
XLA Ops:
  6.5 0.0 copy-start.2
  6.5 4.8 %all-to-all-start = ((bf16[4,48,512]{2,1,0:T(8,128)(2,1)}), bf16[4,48,512]{2,1,0:T(8,128)(2,1)S(1)}, u32[]{:S(2)}, u32[]{:S(2)}) async-start(bf16[4,48,512]{2,1,0:T(8,128)(2,1)} %bitcast.15), calls=%async_computation | async-start | bytes 393216 | tf_op jit(solution)/shard_map/all_to_all | solution.py:145
  11.3 0.0 all-gather.2.cloned.1.call-start
  11.3 0.0 copy-start.1
  11.3 0.9 copy-done.1
  12.3 0.0 copy-start.3
  12.3 0.9 copy-done.3
  13.2 0.0 copy-start.4
  13.2 0.0 copy-start.5
  13.2 0.9 block_state.1
  14.2 1.2 all-to-all-done
  15.4 0.0 copy-start.6
  15.4 0.7 copy-done.6
  16.1 0.0 all-gather.2.cloned.1.call-update
  16.1 10.0 %all-to-all-start.1 = ((bf16[8,64,128]{2,1,0:T(8,128)(2,1)}), bf16[8,64,128]{2,1,0:T(8,128)(2,1)S(1)}, u32[]{:S(2)}, u32[]{:S(2)}) async-start(bf16[8,64,128]{2,1,0:T(8,128)(2,1)} %bitcast.4), calls=%async_computation.1 | async-start | bytes 262144 | tf_op jit(solution)/shard_map/all_to_all | solution.py:130
  26.1 5.8 %all-to-all-done.1 = bf16[8,64,128]{2,1,0:T(8,128)(2,1)S(1)} async-done(((bf16[8,64,128]{2,1,0:T(8,128)(2,1)}), bf16[8,64,128]{2,1,0:T(8,128)(2,1)S(1)}, u32[]{:S(2)}, u32[]{:S(2)}) %all-to-all-start.1) | async-done | bytes 131104 | tf_op jit(solution)/shard_map/all_to_all | solution.py:130
  31.9 17.8 %all_gather.8 = bf16[4,64,128]{2,1,0:T(8,128)(2,1)S(1)} all-gather(bf16[1,64,128]{2,1,0:T(8,128)(2,1)S(1)} %slice.7), channel_id=1, replica_groups=mesh['za'=4,'zb'=2,'zc'=2,'core'=2,'y'=4,'xh'=2,'xl'=2] {'za'}, dimensions={0}, use_global_device_ids=true | all-gather | bytes 81920 | tf_op jit(solution)/shard_map/all_gather | solution.py:134
  49.7 0.1 select_reduce_fusion
  49.8 0.7 fusion.3
  50.5 7.4 %all-to-all-start.2 = ((bf16[8,64,128]{2,1,0:T(8,128)(2,1)}), bf16[8,64,128]{2,1,0:T(8,128)(2,1)S(1)}, u32[]{:S(2)}, u32[]{:S(2)}) async-start(bf16[8,64,128]{2,1,0:T(8,128)(2,1)} %fusion.3), calls=%async_computation.2 | async-start | bytes 262144 | tf_op jit(solution)/shard_map/all_to_all | solution.py:138
  57.9 8.2 %all-to-all-done.2 = bf16[8,64,128]{2,1,0:T(8,128)(2,1)S(1)} async-done(((bf16[8,64,128]{2,1,0:T(8,128)(2,1)}), bf16[8,64,128]{2,1,0:T(8,128)(2,1)S(1)}, u32[]{:S(2)}, u32[]{:S(2)}) %all-to-all-start.2) | async-done | bytes 131104 | tf_op jit(solution)/shard_map/all_to_all | solution.py:138
  66.0 0.0 copy-done.2
  66.1 0.0 copy-done.4
  66.1 0.0 copy-done.5
  66.1 0.8 attend.1
  66.8 23.3 %all_to_all.25 = bf16[4,512,256]{2,1,0:T(8,128)(2,1)S(1)} all-to-all(bf16[4,512,256]{2,1,0:T(8,128)(2,1)S(1)} %attend.1), channel_id=1, replica_groups=mesh['za'=4,'zb'=2,'zc'=2,'core'=2,'y'=4,'xh'=2,'xl'=2] {'zc','xl'}, dimensions={0} | all-to-all | bytes 2097152 | tf_op jit(solution)/shard_map/all_to_all | solution.py:155
  90.1 0.0 all-gather.2.cloned.1.call-done.w_ref
  90.1 0.0 copy-start
  90.1 1.9 %copy-done = bf16[192,8192]{1,0:T(8,128)(2,1)S(1)} copy-done((bf16[192,8192]{1,0:T(8,128)(2,1)S(1)}, bf16[192,8192]{1,0:T(8,128)(2,1)}, u32[]{:S(2)}) %copy-start) | copy-done | bytes 3145752
  92.0 1.8 %project.1 = bf16[2,8,2,2,48,256]{5,4,3,2,1,0:T(8,128)(2,1)S(1)} custom-call(bf16[192,8192]{1,0:T(8,128)(2,1)S(1)} %copy-done, bf16[2,2,512,256]{3,2,1,0:T(8,128)(2,1)S(1)} %bitcast.12), custom_call_target="tpu_custom_call" | custom-call | tf_op jit(solution)/shard_map/project/pallas_call | solution.py:89
  93.8 28.3 %all_to_all.26 = bf16[32,96,256]{2,1,0:T(8,128)(2,1)S(1)} all-to-all(bf16[32,96,256]{2,1,0:T(8,128)(2,1)S(1)} %bitcast.11), channel_id=1, replica_groups=mesh['za'=4,'zb'=2,'zc'=2,'core'=2,'y'=4,'xh'=2,'xl'=2] {'zc','y','xh','..., dimensions={0} | all-to-all | bytes 3145728 | tf_op jit(solution)/shard_map/all_to_all | solution.py:158
  122.1 0.9 finish.1
  (3 shorter events, 0.0 us)
Async XLA Ops:
  6.5 59.5 %copy-start.2 = (bf16[256,512]{1,0:T(8,128)(2,1)S(1)}, bf16[256,512]{1,0:T(8,128)(2,1)}, u32[]{:S(2)}) copy-start(bf16[256,512]{1,0:T(8,128)(2,1)} %k_ref.3) | copy-start | bytes 786436
  6.5 8.8 %all-to-all-start = ((bf16[4,48,512]{2,1,0:T(8,128)(2,1)}), bf16[4,48,512]{2,1,0:T(8,128)(2,1)S(1)}, u32[]{:S(2)}, u32[]{:S(2)}) async-start(bf16[4,48,512]{2,1,0:T(8,128)(2,1)} %bitcast.15), calls=%async_computation | async-start | bytes 393216 | tf_op jit(solution)/shard_map/all_to_all | solution.py:145
  11.3 78.8 %all-gather.2.cloned.1.call-start = ((), (), s32[]{:S(2)}) async-start(), calls=%async_computation.5 | async-start | bytes 3342336 | tf_op jit(solution)/shard_map/all_gather | solution.py:149
  11.3 0.9 copy-start.1
  12.3 0.9 copy-start.3
  13.2 52.8 %copy-start.4 = (bf16[256,512]{1,0:T(8,128)(2,1)S(1)}, bf16[256,512]{1,0:T(8,128)(2,1)}, u32[]{:S(2)}) copy-start(bf16[256,512]{1,0:T(8,128)(2,1)} %v_ref.3) | copy-start | bytes 786436
  13.2 52.8 %copy-start.5 = (bf16[256,512]{1,0:T(8,128)(2,1)S(1)}, bf16[256,512]{1,0:T(8,128)(2,1)}, u32[]{:S(2)}) copy-start(bf16[256,512]{1,0:T(8,128)(2,1)} %q_ref.1) | copy-start | bytes 786436
  15.4 0.7 copy-start.6
  16.1 15.8 %all-to-all-start.1 = ((bf16[8,64,128]{2,1,0:T(8,128)(2,1)}), bf16[8,64,128]{2,1,0:T(8,128)(2,1)S(1)}, u32[]{:S(2)}, u32[]{:S(2)}) async-start(bf16[8,64,128]{2,1,0:T(8,128)(2,1)} %bitcast.4), calls=%async_computation.1 | async-start | bytes 262144 | tf_op jit(solution)/shard_map/all_to_all | solution.py:130
  50.5 15.5 %all-to-all-start.2 = ((bf16[8,64,128]{2,1,0:T(8,128)(2,1)}), bf16[8,64,128]{2,1,0:T(8,128)(2,1)S(1)}, u32[]{:S(2)}, u32[]{:S(2)}) async-start(bf16[8,64,128]{2,1,0:T(8,128)(2,1)} %fusion.3), calls=%async_computation.2 | async-start | bytes 262144 | tf_op jit(solution)/shard_map/all_to_all | solution.py:138
  90.1 1.9 %copy-start = (bf16[192,8192]{1,0:T(8,128)(2,1)S(1)}, bf16[192,8192]{1,0:T(8,128)(2,1)}, u32[]{:S(2)}) copy-start(bf16[192,8192]{1,0:T(8,128)(2,1)} %all-gather.2.cloned.1.call-done.w_ref) | copy-start | bytes 9437188
Sparse Core Ops, SparseCore 0:
  16.2 68.1 all-gather.1

commit v10 on v9

--- a/solution.py
+++ b/solution.py
@@ -76,7 +76,7 @@
                 total = jnp.zeros((pairs * columns, tokens), F32)
                 for g in range(groups):
                     row = (end * groups + g) * columns
-                    lanes = [(pair * halves + half) * width for pair in range(pairs)]
+                    lanes = [(half * pairs + pair) * width for pair in range(pairs)]
                     parts = [w_ref[row : row + columns, lane : lane + width] for lane in lanes]
                     total += dot(jnp.concatenate(parts, axis=0), a_ref[t, g], ((1,), (0,)))
                 out_ref[t, :, end, half] = total.astype(BF16).reshape(pairs, columns, -1)
@@ -146,7 +146,7 @@
     states = block_states(keys, values)
     weight, states = lax.optimization_barrier((weight, states))
     weight = weight.reshape(groups * columns, width)
-    weight = lax.all_gather(weight, ("za", "zb", "core"), axis=1, tiled=True)
+    weight = lax.all_gather(weight, ("core", "za", "zb"), axis=1, tiled=True)
 
     index = lax.axis_index(CTX).astype(jnp.int32).reshape(1)
 

time: 131 us -> 131 us (level)
  no operation moved by 1% of the time
where the time goes in v10:
time: 131 us; the launch traced here: 130 us
  blocking collectives  69.4 us (53%)
  starting transfers between devices  22.2 us (17%)
  waiting for transfers between devices  15.2 us (12%)
  between operations  13.4 us (10%)
  local copies, waits for them, and re-layouts  4.48 us (3%)
  Pallas kernels  4.42 us (3%)
    all_to_all x1, blocking collectives, per_device(): lax.all_to_all(partial.reshape(32, 2 * columns, tokens), ('zc',) + HEAD,...  28.3 us
    all_to_all x1, blocking collectives, per_device(): attended = lax.all_to_all(attended, PAIRS, 0, 0)  23.2 us
    all_gather x1, blocking collectives, earlier_states(): totals = lax.all_gather(total.astype(BF16), FAR).astype(F32)  17.8 us
    all_to_all x1, starting transfers between devices, earlier_states(): lax.all_to_all(state.reshape(near, state.shape[0] // near, DH), NEAR, 0, 0)  9.99 us
    all_to_all x1, waiting for transfers between devices, earlier_states(): return lax.all_to_all(prefix, NEAR, 0, 0).reshape(state.shape)  8.14 us
    all_to_all x1, starting transfers between devices, earlier_states(): return lax.all_to_all(prefix, NEAR, 0, 0).reshape(state.shape)  7.37 us
    all_to_all x1, waiting for transfers between devices, earlier_states(): lax.all_to_all(state.reshape(near, state.shape[0] // near, DH), NEAR, 0, 0)  5.84 us
    all_to_all x1, starting transfers between devices, per_device(): lax.all_to_all(out_weight.T.reshape(groups, columns, width), PAIRS, 0, 0)  4.79 us
  transfers between devices with their start and end apart: 4, of which 3 were waited for; matrix products, arithmetic and copies ran while one was open for 1% of the time, Pallas kernels for 1%

profile of v10, /device:TPU:1, one launch (start us, length us, event | category | flops | bytes accessed | tf_op | source)
XLA Modules:
  0.0 129.9 jit_solution(9930574472768134800)
XLA Ops:
  6.5 0.0 copy-start.2
  6.5 4.8 %all-to-all-start = ((bf16[4,48,512]{2,1,0:T(8,128)(2,1)}), bf16[4,48,512]{2,1,0:T(8,128)(2,1)S(1)}, u32[]{:S(2)}, u32[]{:S(2)}) async-start(bf16[4,48,512]{2,1,0:T(8,128)(2,1)} %bitcast.15), calls=%async_computation | async-start | bytes 393216 | tf_op jit(solution)/shard_map/all_to_all | solution.py:145
  11.3 0.0 all-gather.2.cloned.1.call-start
  11.3 0.0 copy-start.1
  11.3 0.9 copy-done.1
  12.3 0.0 copy-start.3
  12.3 0.9 copy-done.3
  13.2 0.0 copy-start.4
  13.2 0.0 copy-start.5
  13.2 0.9 block_state.1
  14.2 1.2 all-to-all-done
  15.4 0.0 copy-start.6
  15.4 0.7 copy-done.6
  16.1 0.0 all-gather.2.cloned.1.call-update
  16.1 10.0 %all-to-all-start.1 = ((bf16[8,64,128]{2,1,0:T(8,128)(2,1)}), bf16[8,64,128]{2,1,0:T(8,128)(2,1)S(1)}, u32[]{:S(2)}, u32[]{:S(2)}) async-start(bf16[8,64,128]{2,1,0:T(8,128)(2,1)} %bitcast.4), calls=%async_computation.1 | async-start | bytes 262144 | tf_op jit(solution)/shard_map/all_to_all | solution.py:130
  26.1 5.8 %all-to-all-done.1 = bf16[8,64,128]{2,1,0:T(8,128)(2,1)S(1)} async-done(((bf16[8,64,128]{2,1,0:T(8,128)(2,1)}), bf16[8,64,128]{2,1,0:T(8,128)(2,1)S(1)}, u32[]{:S(2)}, u32[]{:S(2)}) %all-to-all-start.1) | async-done | bytes 131104 | tf_op jit(solution)/shard_map/all_to_all | solution.py:130
  31.9 17.8 %all_gather.8 = bf16[4,64,128]{2,1,0:T(8,128)(2,1)S(1)} all-gather(bf16[1,64,128]{2,1,0:T(8,128)(2,1)S(1)} %slice.7), channel_id=1, replica_groups=mesh['za'=4,'zb'=2,'zc'=2,'core'=2,'y'=4,'xh'=2,'xl'=2] {'za'}, dimensions={0}, use_global_device_ids=true | all-gather | bytes 81920 | tf_op jit(solution)/shard_map/all_gather | solution.py:134
  49.7 0.1 select_reduce_fusion
  49.8 0.7 fusion.3
  50.5 7.4 %all-to-all-start.2 = ((bf16[8,64,128]{2,1,0:T(8,128)(2,1)}), bf16[8,64,128]{2,1,0:T(8,128)(2,1)S(1)}, u32[]{:S(2)}, u32[]{:S(2)}) async-start(bf16[8,64,128]{2,1,0:T(8,128)(2,1)} %fusion.3), calls=%async_computation.2 | async-start | bytes 262144 | tf_op jit(solution)/shard_map/all_to_all | solution.py:138
  57.9 8.1 %all-to-all-done.2 = bf16[8,64,128]{2,1,0:T(8,128)(2,1)S(1)} async-done(((bf16[8,64,128]{2,1,0:T(8,128)(2,1)}), bf16[8,64,128]{2,1,0:T(8,128)(2,1)S(1)}, u32[]{:S(2)}, u32[]{:S(2)}) %all-to-all-start.2) | async-done | bytes 131104 | tf_op jit(solution)/shard_map/all_to_all | solution.py:138
  66.0 0.0 copy-done.2
  66.0 0.0 copy-done.4
  66.0 0.0 copy-done.5
  66.0 0.8 attend.1
  66.8 23.2 %all_to_all.25 = bf16[4,512,256]{2,1,0:T(8,128)(2,1)S(1)} all-to-all(bf16[4,512,256]{2,1,0:T(8,128)(2,1)S(1)} %attend.1), channel_id=1, replica_groups=mesh['za'=4,'zb'=2,'zc'=2,'core'=2,'y'=4,'xh'=2,'xl'=2] {'zc','xl'}, dimensions={0} | all-to-all | bytes 2097152 | tf_op jit(solution)/shard_map/all_to_all | solution.py:155
  90.0 0.0 all-gather.2.cloned.1.call-done.w_ref
  90.0 0.0 copy-start
  90.1 1.9 %copy-done = bf16[192,8192]{1,0:T(8,128)(2,1)S(1)} copy-done((bf16[192,8192]{1,0:T(8,128)(2,1)S(1)}, bf16[192,8192]{1,0:T(8,128)(2,1)}, u32[]{:S(2)}) %copy-start) | copy-done | bytes 3145752
  91.9 1.8 %project.1 = bf16[2,8,2,2,48,256]{5,4,3,2,1,0:T(8,128)(2,1)S(1)} custom-call(bf16[192,8192]{1,0:T(8,128)(2,1)S(1)} %copy-done, bf16[2,2,512,256]{3,2,1,0:T(8,128)(2,1)S(1)} %bitcast.12), custom_call_target="tpu_custom_call" | custom-call | tf_op jit(solution)/shard_map/project/pallas_call | solution.py:89
  93.7 28.3 %all_to_all.26 = bf16[32,96,256]{2,1,0:T(8,128)(2,1)S(1)} all-to-all(bf16[32,96,256]{2,1,0:T(8,128)(2,1)S(1)} %bitcast.11), channel_id=1, replica_groups=mesh['za'=4,'zb'=2,'zc'=2,'core'=2,'y'=4,'xh'=2,'xl'=2] {'zc','y','xh','..., dimensions={0} | all-to-all | bytes 3145728 | tf_op jit(solution)/shard_map/all_to_all | solution.py:158
  122.1 0.9 finish.1
  (3 shorter events, 0.0 us)
Async XLA Ops:
  6.5 59.5 %copy-start.2 = (bf16[256,512]{1,0:T(8,128)(2,1)S(1)}, bf16[256,512]{1,0:T(8,128)(2,1)}, u32[]{:S(2)}) copy-start(bf16[256,512]{1,0:T(8,128)(2,1)} %k_ref.3) | copy-start | bytes 786436
  6.5 8.8 %all-to-all-start = ((bf16[4,48,512]{2,1,0:T(8,128)(2,1)}), bf16[4,48,512]{2,1,0:T(8,128)(2,1)S(1)}, u32[]{:S(2)}, u32[]{:S(2)}) async-start(bf16[4,48,512]{2,1,0:T(8,128)(2,1)} %bitcast.15), calls=%async_computation | async-start | bytes 393216 | tf_op jit(solution)/shard_map/all_to_all | solution.py:145
  11.3 78.7 %all-gather.2.cloned.1.call-start = ((), (), s32[]{:S(2)}) async-start(), calls=%async_computation.5 | async-start | bytes 3342336 | tf_op jit(solution)/shard_map/all_gather | solution.py:149
  11.3 0.9 copy-start.1
  12.3 0.9 copy-start.3
  13.2 52.8 %copy-start.4 = (bf16[256,512]{1,0:T(8,128)(2,1)S(1)}, bf16[256,512]{1,0:T(8,128)(2,1)}, u32[]{:S(2)}) copy-start(bf16[256,512]{1,0:T(8,128)(2,1)} %v_ref.3) | copy-start | bytes 786436
  13.2 52.8 %copy-start.5 = (bf16[256,512]{1,0:T(8,128)(2,1)S(1)}, bf16[256,512]{1,0:T(8,128)(2,1)}, u32[]{:S(2)}) copy-start(bf16[256,512]{1,0:T(8,128)(2,1)} %q_ref.1) | copy-start | bytes 786436
  15.4 0.7 copy-start.6
  16.1 15.8 %all-to-all-start.1 = ((bf16[8,64,128]{2,1,0:T(8,128)(2,1)}), bf16[8,64,128]{2,1,0:T(8,128)(2,1)S(1)}, u32[]{:S(2)}, u32[]{:S(2)}) async-start(bf16[8,64,128]{2,1,0:T(8,128)(2,1)} %bitcast.4), calls=%async_computation.1 | async-start | bytes 262144 | tf_op jit(solution)/shard_map/all_to_all | solution.py:130
  50.5 15.5 %all-to-all-start.2 = ((bf16[8,64,128]{2,1,0:T(8,128)(2,1)}), bf16[8,64,128]{2,1,0:T(8,128)(2,1)S(1)}, u32[]{:S(2)}, u32[]{:S(2)}) async-start(bf16[8,64,128]{2,1,0:T(8,128)(2,1)} %fusion.3), calls=%async_computation.2 | async-start | bytes 262144 | tf_op jit(solution)/shard_map/all_to_all | solution.py:138
  90.0 1.9 %copy-start = (bf16[192,8192]{1,0:T(8,128)(2,1)S(1)}, bf16[192,8192]{1,0:T(8,128)(2,1)}, u32[]{:S(2)}) copy-start(bf16[192,8192]{1,0:T(8,128)(2,1)} %all-gather.2.cloned.1.call-done.w_ref) | copy-start | bytes 9437188
Sparse Core Ops, SparseCore 0:
  16.2 68.7 all-gather.1
